TPU v7x, 32 devices: a whole 2x2x4 slice. The times are simulated.
32 devices in a mesh: lat: 4 (over y, core), lon: 8 (over z, x).
Axes of the slice: x: 2, y: 2, z: 4, core: 2. Of those that a mesh axis runs over, the one named last changes fastest.
Arguments:
- residual: bfloat16 [128, 128, 128], P('lat', 'lon'), may hold values from -6 to 6
- noise_weights: float32 [128, 128], P('lat', 'lon'), may hold values from 0.5 to 4
- kernel: bfloat16 [4, 1, 2048, 2048], P(None, None, 'lat'), may hold values from -0.0625 to 0.0625
Outputs:
- gradient: float32 [1, 128, 128, 128], P(None, 'lat', 'lon')
All inputs are finite; a program needn't handle non-finite values.
Results may differ from a plain program's by a relative error of at most 0.0029.
Values may be sent and summed in bfloat16 or wider, within the bound.
A program may use at most 64 MiB of HBM per device.

v0:
```python
import jax
import jax.numpy as jnp
from jax import lax
from jax.sharding import PartitionSpec as P


def shifted(value, axis, by):
    length = lax.axis_size(axis)
    return lax.ppermute(value, axis, [(i, (i + by) % length) for i in range(length)])


def contribution(kernel_slab, weighted):
    return jnp.einsum("lqc,qp->lcp", kernel_slab, weighted, preferred_element_type=jnp.float32)


def per_device(residual, noise_weights, kernel):
    offsets = kernel.shape[0]
    obs_rows = residual.shape[0] * residual.shape[1]
    weighted = (noise_weights[:, :, None] * residual.astype(jnp.float32)).astype(jnp.bfloat16)
    weighted = weighted.reshape(obs_rows, residual.shape[2])
    carried = contribution(kernel[offsets - 1], weighted)
    for offset in range(offsets - 2, -1, -1):
        carried = shifted(carried, "lon", 1) + contribution(kernel[offset], weighted)
    owned_sums = lax.psum_scatter(carried, "lat", scatter_dimension=1, tiled=True)
    return owned_sums.reshape(
        kernel.shape[1], residual.shape[0], residual.shape[1], residual.shape[2]
    )


def solution(mesh):
    return jax.shard_map(
        per_device,
        mesh=mesh,
        in_specs=(P("lat", "lon", None), P("lat", "lon"), P(None, None, "lat", None)),
        out_specs=P(None, "lat", "lon", None),
        check_vma=False,
    )
```

profile of v0, /device:TPU:1, one launch (start us, length us, event | category | flops | bytes accessed | tf_op | source)
XLA Modules:
  0.0 126.1 jit_solution(12966894985575756271)
XLA Ops:
  6.5 0.0 reduce-scatter.2.cloned.1.call-start
  6.5 0.8 copy.6
  7.3 1.0 multiply_convert_fusion
  8.3 2.1 %convolution_bitcast_fusion.3 = f32[1,2048,128]{1,2,0:T(8,128)S(1)} fusion(bf16[512,128]{1,0:T(8,128)(2,1)S(1)} %bitcast.36, bf16[4,1,512,2048]{3,2,1,0:T(8,128)(2,1)} %param.5), kind=kOutput, calls=%fused_computation.3 | convolution fusion | flops 268435456 | bytes 3276800 | tf_op jit(solution)/shard_map/lqc,qp->lcp/dot_general | solution.py:13
  10.4 2.1 %collective-permute-start = (f32[1,2048,128]{1,2,0:T(8,128)S(1)}, f32[1,2048,128]{1,2,0:T(8,128)S(1)}, u32[]{:S(2)}, u32[]{:S(2)}) collective-permute-start(f32[1,2048,128]{1,2,0:T(8,128)S(1)} %convolution_bitcast_fusion.3), channel_id=1, source_target_pairs={{0,1},{1,2},{2,3},{3,4},{4,5},{5,6},{6,7},{7,0},{8,9},{9,10},{10,1... | collective-permute-start | bytes 3145736 | tf_op jit(solution)/shard_map/ppermute | solution.py:9
  12.5 25.9 %collective-permute-done = f32[1,2048,128]{1,2,0:T(8,128)S(1)} collective-permute-done((f32[1,2048,128]{1,2,0:T(8,128)S(1)}, f32[1,2048,128]{1,2,0:T(8,128)S(1)}, u32[]{:S(2)}, u32[]{:S(2)}) %collective-permute-start) | collective-permute-done | bytes 1048608 | tf_op jit(solution)/shard_map/ppermute | solution.py:9
  38.4 2.1 %fusion = f32[1,2048,128]{1,2,0:T(8,128)S(1)} fusion(f32[1,2048,128]{1,2,0:T(8,128)S(1)} %collective-permute-done, bf16[512,128]{1,0:T(8,128)(2,1)S(1)} %bitcast.37, bf16[4,1,512,2048]{3,2,1,0:T(8,128)(2,1)} %param.5), kind=kOutput, calls=%fused_computation.4 | convolution fusion | flops 268697600 | bytes 4325376 | tf_op jit(solution)/shard_map/lqc,qp->lcp/dot_general | solution.py:13
  40.5 0.1 collective-permute-start.1
  40.5 2.1 %convolution_bitcast_fusion.1 = f32[1,2048,128]{1,2,0:T(8,128)S(1)} fusion(bf16[512,128]{1,0:T(8,128)(2,1)S(1)} %bitcast.38, bf16[4,1,512,2048]{3,2,1,0:T(8,128)(2,1)} %param.5), kind=kOutput, calls=%fused_computation.1 | convolution fusion | flops 268435456 | bytes 3276800 | tf_op jit(solution)/shard_map/lqc,qp->lcp/dot_general | solution.py:13
  42.6 24.0 %collective-permute-done.1 = f32[1,2048,128]{1,2,0:T(8,128)S(1)} collective-permute-done((f32[1,2048,128]{1,2,0:T(8,128)S(1)}, f32[1,2048,128]{1,2,0:T(8,128)S(1)}, u32[]{:S(2)}, u32[]{:S(2)}) %collective-permute-start.1) | collective-permute-done | bytes 1048608 | tf_op jit(solution)/shard_map/ppermute | solution.py:9
  66.6 0.1 add.12
  66.8 0.1 collective-permute-start.2
  66.8 2.1 %convolution_bitcast_fusion = f32[1,2048,128]{1,2,0:T(8,128)S(1)} fusion(bf16[512,128]{1,0:T(8,128)(2,1)S(1)} %bitcast.39, bf16[4,1,512,2048]{3,2,1,0:T(8,128)(2,1)} %param.5), kind=kOutput, calls=%fused_computation | convolution fusion | flops 268435456 | bytes 3276800 | tf_op jit(solution)/shard_map/lqc,qp->lcp/dot_general | solution.py:13
  68.9 23.1 %collective-permute-done.2 = f32[1,2048,128]{1,2,0:T(8,128)S(1)} collective-permute-done((f32[1,2048,128]{1,2,0:T(8,128)S(1)}, f32[1,2048,128]{1,2,0:T(8,128)S(1)}, u32[]{:S(2)}, u32[]{:S(2)}) %collective-permute-start.2) | collective-permute-done | bytes 1048608 | tf_op jit(solution)/shard_map/ppermute | solution.py:9
  92.0 1.1 add.13
  93.1 0.0 reduce-scatter.2.cloned.1.call-update
  93.1 24.3 %reduce-scatter.2.cloned.1.call-done = f32[1,512,128]{1,2,0:T(8,128)} async-done(((f32[1,2048,128]{1,2,0:T(8,128)}), f32[1,512,128]{1,2,0:T(8,128)}) %reduce-scatter.2.cloned.1.call-update) | async-done | bytes 262160 | tf_op jit(solution)/shard_map/reduce_scatter | solution.py:24
  117.4 1.8 %copy.7 = f32[1,512,128]{2,1,0:T(8,128)} copy(f32[1,512,128]{1,2,0:T(8,128)} %reduce-scatter.2.cloned.1.call-done) | data formatting | bytes 524288 | tf_op jit(solution)/shard_map/reduce_scatter | solution.py:24
Async XLA Ops:
  6.5 110.9 %reduce-scatter.2.cloned.1.call-start = ((), (), s32[]{:S(2)}) async-start(), calls=%async_computation.1 | async-start | bytes 1310720 | tf_op jit(solution)/shard_map/reduce_scatter | solution.py:24
  10.4 28.0 %collective-permute-start = (f32[1,2048,128]{1,2,0:T(8,128)S(1)}, f32[1,2048,128]{1,2,0:T(8,128)S(1)}, u32[]{:S(2)}, u32[]{:S(2)}) collective-permute-start(f32[1,2048,128]{1,2,0:T(8,128)S(1)} %convolution_bitcast_fusion.3), channel_id=1, source_target_pairs={{0,1},{1,2},{2,3},{3,4},{4,5},{5,6},{6,7},{7,0},{8,9},{9,10},{10,1... | collective-permute-start | bytes 3145736 | tf_op jit(solution)/shard_map/ppermute | solution.py:9
  40.5 26.2 %collective-permute-start.1 = (f32[1,2048,128]{1,2,0:T(8,128)S(1)}, f32[1,2048,128]{1,2,0:T(8,128)S(1)}, u32[]{:S(2)}, u32[]{:S(2)}) collective-permute-start(f32[1,2048,128]{1,2,0:T(8,128)S(1)} %fusion), channel_id=1, source_target_pairs={{0,1},{1,2},{2,3},{3,4},{4,5},{5,6},{6,7},{7,0},{8,9},{9,10},{10,1... | collective-permute-start | bytes 3145736 | tf_op jit(solution)/shard_map/ppermute | solution.py:9
  66.8 25.2 %collective-permute-start.2 = (f32[1,2048,128]{1,2,0:T(8,128)S(1)}, f32[1,2048,128]{1,2,0:T(8,128)S(1)}, u32[]{:S(2)}, u32[]{:S(2)}) collective-permute-start(f32[1,2048,128]{1,2,0:T(8,128)S(1)} %add.12), channel_id=1, source_target_pairs={{0,1},{1,2},{2,3},{3,4},{4,5},{5,6},{6,7},{7,0},{8,9},{9,10},{10,1... | collective-permute-start | bytes 3145736 | tf_op jit(solution)/shard_map/ppermute | solution.py:9
Sparse Core Ops, SparseCore 0:
  93.2 24.1 reduce-scatter.1
where the time goes:
time: 127 us; the launch traced here: 126 us
  waiting for transfers between devices  97.4 us (77%)
  between operations  13.4 us (11%)
  matrix products  8.22 us (6%)
  local copies, waits for them, and re-layouts  2.55 us (2%)
  other arithmetic  2.25 us (2%)
  starting transfers between devices  2.22 us (2%)
    ppermute x3, waiting for transfers between devices, shifted(): lax.ppermute(value, axis, [(i, (i + by) % length) for i in range(length)])  73.1 us
    reduce_scatter x1, waiting for transfers between devices, per_device(): lax.psum_scatter(carried, 'lat', scatter_dimension=1, tiled=True)  24.3 us
    dot_general x4, matrix products, contribution(): jnp.einsum('lqc,qp->lcp', kernel_slab, weighted, preferred_element_type=j...  8.22 us
  transfers between devices with their start and end apart: 4, of which 4 were waited for; matrix products, arithmetic and copies ran while one was open for 3% of the time, Pallas kernels for 0%

commit v1 on v0

v1 whole, which is shorter than its diff:
```python
import functools

import jax
import jax.numpy as jnp
from jax import lax
from jax.experimental import pallas as pl
from jax.experimental.pallas import tpu as pltpu
from jax.sharding import PartitionSpec as P

MESH = pl.DeviceIdType.MESH


def sweep(
    lats, lons, res_ref, nw_ref, panel_hbm, out_ref,
    panel, blocks, total, outgoing, incoming,
    panel_sem, east_send, east_recv, band_send, band_recv,
):
    offsets, layers, rows, cells = panel_hbm.shape
    probes = res_ref.shape[-1]
    band = cells // lats
    lat, lon = lax.axis_index("lat"), lax.axis_index("lon")

    loads = []
    for d in range(offsets):
        for l in range(layers):
            load = pltpu.make_async_copy(
                panel_hbm.at[d, l], panel.at[d, l], panel_sem.at[d, l]
            )
            load.start()
            loads.append(load)

    barrier = pltpu.get_barrier_semaphore()
    for d in range(1, offsets):
        pl.semaphore_signal(
            barrier, inc=1, device_id=(lat, lax.rem(lon + lons - d, lons)), device_id_type=MESH
        )
    for s in range(1, lats):
        pl.semaphore_signal(
            barrier, inc=1, device_id=(lax.rem(lat + s, lats), lon), device_id_type=MESH
        )

    weighted = nw_ref[...][:, :, None] * res_ref[...].astype(jnp.float32)
    blocks[0] = weighted.reshape(rows, probes).T.astype(jnp.bfloat16)

    pl.semaphore_wait(barrier, offsets - 1 + lats - 1)
    east = []
    for d in range(1, offsets):
        copy = pltpu.make_async_remote_copy(
            src_ref=blocks.at[0],
            dst_ref=blocks.at[d],
            send_sem=east_send.at[d - 1],
            recv_sem=east_recv.at[d - 1],
            device_id=(lat, lax.rem(lon + d, lons)),
            device_id_type=MESH,
        )
        copy.start()
        east.append(copy)

    def term(d, l, first):
        columns = pl.ds(pl.multiple_of(first, band), band)
        return columns, jnp.dot(
            blocks[d], panel[d, l, :, columns], preferred_element_type=jnp.float32
        )

    for d in range(offsets - 1):
        for l in range(layers):
            loads[d * layers + l].wait()
        if d > 0:
            east[d - 1].wait_recv()
        for l in range(layers):
            for b in range(lats):
                columns, value = term(d, l, b * band)
                if d == 0:
                    total[l, :, columns] = value
                else:
                    total[l, :, columns] += value

    last = offsets - 1
    for l in range(layers):
        loads[last * layers + l].wait()
    east[last - 1].wait_recv()
    sent = []
    for s in range(1, lats):
        to = lax.rem(lat + s, lats)
        for l in range(layers):
            columns, value = term(last, l, to * band)
            outgoing[s - 1, l] = (total[l, :, columns] + value).astype(jnp.bfloat16)
        copy = pltpu.make_async_remote_copy(
            src_ref=outgoing.at[s - 1],
            dst_ref=incoming.at[s - 1],
            send_sem=band_send.at[s - 1],
            recv_sem=band_recv.at[s - 1],
            device_id=(to, lon),
            device_id_type=MESH,
        )
        copy.start()
        sent.append(copy)
    own = []
    for l in range(layers):
        columns, value = term(last, l, lat * band)
        own.append(total[l, :, columns] + value)
    for copy in sent:
        copy.wait_recv()
    for l in range(layers):
        value = own[l]
        for s in range(1, lats):
            value = value + incoming[s - 1, l].astype(jnp.float32)
        out_ref[l] = value.T.reshape(out_ref.shape[1:])
    for copy in east + sent:
        copy.wait_send()


def per_device(lats, lons, residual, noise_weights, kernel):
    offsets, layers, rows, cells = kernel.shape
    probes = residual.shape[2]
    band = cells // lats
    vmem = pl.BlockSpec(memory_space=pltpu.VMEM)
    return pl.pallas_call(
        functools.partial(sweep, lats, lons),
        out_shape=jax.ShapeDtypeStruct(
            (layers, residual.shape[0], residual.shape[1], probes), jnp.float32
        ),
        in_specs=[vmem, vmem, pl.BlockSpec(memory_space=pl.ANY)],
        out_specs=vmem,
        scratch_shapes=[
            pltpu.VMEM((offsets, layers, rows, cells), jnp.bfloat16),
            pltpu.VMEM((offsets, probes, rows), jnp.bfloat16),
            pltpu.VMEM((layers, probes, cells), jnp.float32),
            pltpu.VMEM((lats - 1, layers, probes, band), jnp.bfloat16),
            pltpu.VMEM((lats - 1, layers, probes, band), jnp.bfloat16),
            pltpu.SemaphoreType.DMA((offsets, layers)),
            pltpu.SemaphoreType.DMA((offsets - 1,)),
            pltpu.SemaphoreType.DMA((offsets - 1,)),
            pltpu.SemaphoreType.DMA((lats - 1,)),
            pltpu.SemaphoreType.DMA((lats - 1,)),
        ],
        compiler_params=pltpu.CompilerParams(
            collective_id=0, has_side_effects=True, vmem_limit_bytes=48 * 1024 * 1024
        ),
        cost_estimate=pl.CostEstimate(
            flops=2 * offsets * layers * rows * cells * probes,
            bytes_accessed=2 * offsets * layers * rows * cells,
            transcendentals=0,
        ),
    )(residual, noise_weights, kernel)


def solution(mesh):
    return jax.shard_map(
        functools.partial(per_device, mesh.shape["lat"], mesh.shape["lon"]),
        mesh=mesh,
        in_specs=(P("lat", "lon", None), P("lat", "lon"), P(None, None, "lat", None)),
        out_specs=P(None, "lat", "lon", None),
        check_vma=False,
    )
```

time: 127 us -> 28.1 us (0.22)
  waiting for transfers between devices: 97.4 us -> 0 us
  Pallas kernels: 0 us -> 25.5 us
  between operations: 13.4 us -> 0.01 us
  matrix products: 8.22 us -> 0 us
  other arithmetic: 2.25 us -> 0 us
  starting transfers between devices: 2.22 us -> 0 us
    ppermute x3 -> x0, waiting for transfers between devices: 73.1 us -> none  [shifted(): lax.ppermute(value, axis, [(i, (i + by) % length) for i in range(length)])]
    pallas_call x0 -> x1, Pallas kernels: none -> 25.5 us  [per_device(): pl.pallas_call(functools.partial(sweep, lats, lons), out_shape=jax.ShapeD...]
    reduce_scatter x1 -> x0, waiting for transfers between devices: 24.3 us -> none  [per_device(): lax.psum_scatter(carried, 'lat', scatter_dimension=1, tiled=True)]
    dot_general x4 -> x0, matrix products: 8.22 us -> none  [contribution(): jnp.einsum('lqc,qp->lcp', kernel_slab, weighted, preferred_element_type=j...]
    ppermute x3 -> x0, starting transfers between devices: 2.21 us -> none  [shifted(): lax.ppermute(value, axis, [(i, (i + by) % length) for i in range(length)])]
    reduce_scatter x1 -> x0, local copies, waits for them, and re-layouts: 1.78 us -> none  [per_device(): lax.psum_scatter(carried, 'lat', scatter_dimension=1, tiled=True)]
    unnamed x1 -> x4, local copies, waits for them, and re-layouts: 0.77 us -> 2.38 us
  transfers between devices with their start and end apart: 4 -> 0, of which waited for: 4 -> 0; matrix products, arithmetic and copies ran while one was open for 3% -> 0% of each run, Pallas kernels for 0% -> 0%
where the time goes in v1:
time: 28.1 us; the launch traced here: 27.9 us
  Pallas kernels  25.5 us (91%)
  local copies, waits for them, and re-layouts  2.38 us (8%)
    pallas_call x1, Pallas kernels, per_device(): pl.pallas_call(functools.partial(sweep, lats, lons), out_shape=jax.ShapeD...  25.5 us
    unnamed x4, local copies, waits for them, and re-layouts  2.38 us

profile of v1, /device:TPU:1, one launch (start us, length us, event | category | flops | bytes accessed | tf_op | source)
XLA Modules:
  0.0 27.9 jit_solution(6343016597229375733)
XLA Ops:
  0.0 0.8 %copy.4.nw_ref = f32[32,16]{1,0:T(8,128)S(1)} copy(f32[32,16]{0,1:T(8,128)} %param.4) | data formatting | bytes 4096 | tf_op args[1]
  0.8 0.0 copy-start
  0.8 0.9 %copy-done = bf16[32,16,128]{2,1,0:T(8,128)(2,1)S(1)} copy-done((bf16[32,16,128]{2,1,0:T(8,128)(2,1)S(1)}, bf16[32,16,128]{2,1,0:T(8,128)(2,1)}, u32[]{:S(2)}) %copy-start) | copy-done | bytes 131096
  1.7 25.5 %shard_map.37 = f32[1,32,16,128]{3,2,1,0:T(8,128)S(1)} custom-call(bf16[32,16,128]{2,1,0:T(8,128)(2,1)S(1)} %copy-done, f32[32,16]{1,0:T(8,128)S(1)} %copy.4.nw_ref, bf16[4,1,512,2048]{3,2,1,0:T(8,128)(2,1)} %panel_hbm.1), custom_call_target="tpu_custom_call" | custom-call | flops 1073741824 | bytes 8388608 | tf_op jit(solution)/shard_map/pallas_call | solution.py:118
  27.2 0.7 %copy.6 = f32[1,32,16,128]{3,2,1,0:T(8,128)} copy(f32[1,32,16,128]{3,2,1,0:T(8,128)S(1)} %shard_map.37) | data formatting | bytes 524288
Async XLA Ops:
  0.8 0.9 %copy-start = (bf16[32,16,128]{2,1,0:T(8,128)(2,1)S(1)}, bf16[32,16,128]{2,1,0:T(8,128)(2,1)}, u32[]{:S(2)}) copy-start(bf16[32,16,128]{2,1,0:T(8,128)(2,1)} %res_ref.1) | copy-start | bytes 393220

commit v2 on v0

v2 whole, which is shorter than its diff:
```python
import functools

import jax
import jax.numpy as jnp
from jax import lax
from jax.experimental import pallas as pl
from jax.experimental.pallas import tpu as pltpu
from jax.sharding import PartitionSpec as P

MESH = pl.DeviceIdType.MESH


def route(offsets, lons):
    if lons % 2 or offsets < 3:
        table = {d: (-d, 0) for d in range(1, offsets)}
        return 1, [table], list(range(1, offsets))
    even, odd = {}, {}
    for d in range(1, offsets):
        even[d] = (1, 2) if d == 1 else (-2, d - 2)
        odd[d] = (-1, d - 1) if d % 2 else (-2, d - 2)
    return 2, [even, odd], list(range(2, offsets, 2)) + list(range(1, offsets, 2))


def sweep(
    lats, lons, res_hbm, nw_hbm, panel_hbm, out_ref,
    res, nw, panel, blocks, total, outgoing, incoming, summed,
    input_sem, panel_sem, east_send, east_recv, band_send, band_recv,
):
    offsets, layers, rows, cells = panel_hbm.shape
    probes = res_hbm.shape[-1]
    chunks, part = outgoing.shape[0], outgoing.shape[3]
    band = cells // lats
    lat, lon = lax.axis_index("lat"), lax.axis_index("lon")
    period, source, order = route(offsets, lons)
    pair = 2 if lats % 2 == 0 else 1
    groups = lats // pair

    res_load = pltpu.make_async_copy(res_hbm, res, input_sem.at[0])
    nw_load = pltpu.make_async_copy(nw_hbm, nw, input_sem.at[1])
    res_load.start()
    nw_load.start()
    loads = {}
    for d in [0] + order:
        loads[d] = pltpu.make_async_copy(panel_hbm.at[d], panel.at[d], panel_sem.at[d])
        loads[d].start()

    def along(delta):
        return (lat, lax.rem(lon + (delta + lons), lons))

    def across(a, b):
        to = lax.rem(lat // pair + a, groups) * pair + lax.rem(lat % pair + b, pair)
        return (to, lon)

    partners = [(a, b) for a in range(groups - 1, -1, -1) for b in range(pair)][: lats]
    partners = [ab for ab in partners if ab != (0, 0)]

    sends = [[] for _ in range(period)]
    senders = [set() for _ in range(period)]
    for q in range(period):
        for d in order:
            delta, held = source[q][d]
            sends[(q + delta) % period].append((-delta, held, d))
            senders[q].add(delta)

    def per_parity(action):
        for q in range(period):
            if period == 1:
                action(q)
            else:
                pl.when(lax.rem(lon, period) == q)(functools.partial(action, q))

    barrier = pltpu.get_barrier_semaphore()

    def greet(q):
        for delta in sorted(senders[q]):
            pl.semaphore_signal(barrier, inc=1, device_id=along(delta), device_id_type=MESH)

    per_parity(greet)
    for a, b in partners:
        pl.semaphore_signal(barrier, inc=1, device_id=across(a, b), device_id_type=MESH)

    res_load.wait()
    nw_load.wait()
    columns = res.shape[1]
    pieces = [
        nw[:, y : y + 1] * res[y].astype(jnp.float32) for y in range(rows // columns)
    ]
    blocks[0] = jnp.concatenate(pieces, axis=0).T.astype(jnp.bfloat16)

    def chunk(c):
        return pl.ds(c * part, part)

    def east(q, n, c):
        delta, held, d = sends[q][n]
        return pltpu.make_async_remote_copy(
            src_ref=blocks.at[held, chunk(c)],
            dst_ref=blocks.at[d, chunk(c)],
            send_sem=east_send.at[n, c],
            recv_sem=east_recv.at[d, c],
            device_id=along(delta),
            device_id_type=MESH,
        )

    def forward(held, cs):
        def action(q):
            for c in cs:
                for n, send in enumerate(sends[q]):
                    if send[1] == held:
                        east(q, n, c).start()

        per_parity(action)

    def arrive(d, c):
        pltpu.make_async_remote_copy(
            src_ref=blocks.at[d, chunk(c)],
            dst_ref=blocks.at[d, chunk(c)],
            send_sem=east_send.at[0, c],
            recv_sem=east_recv.at[d, c],
            device_id=along(1),
            device_id_type=MESH,
        ).wait_recv()

    pl.semaphore_wait(barrier, len(senders[0]) + len(partners))
    forward(0, range(chunks))

    def accumulate(d, first):
        loads[d].wait()
        for l in range(layers):

            @pl.loop(0, lats)
            def _(b):
                cols = pl.ds(pl.multiple_of(b * band, band), band)
                value = jnp.dot(
                    blocks[d], panel[d, l, :, cols], preferred_element_type=jnp.float32
                )
                total[l, :, cols] = value if first else total[l, :, cols] + value

    accumulate(0, True)
    for d in order[:-1]:
        for c in range(chunks):
            arrive(d, c)
            forward(d, [c])
        accumulate(d, False)

    last = order[-1]
    loads[last].wait()

    def finish(c, to):
        cols = pl.ds(pl.multiple_of(to * band, band), band)
        return [
            total[l, chunk(c), cols]
            + jnp.dot(
                blocks[last, chunk(c)], panel[last, l, :, cols],
                preferred_element_type=jnp.float32,
            )
            for l in range(layers)
        ]

    sent = {}
    for c in range(chunks):
        arrive(last, c)
        for n, (a, b) in enumerate(partners):
            to = across(a, b)
            for l, value in enumerate(finish(c, to[0])):
                outgoing[c, n, l] = value.astype(jnp.bfloat16)
            sent[c, n] = pltpu.make_async_remote_copy(
                src_ref=outgoing.at[c, n],
                dst_ref=incoming.at[c, n],
                send_sem=band_send.at[c, n],
                recv_sem=band_recv.at[c, n],
                device_id=to,
                device_id_type=MESH,
            )
            sent[c, n].start()
        for l, value in enumerate(finish(c, lat)):
            summed[l, chunk(c)] = value
    for c in range(chunks):
        for n in reversed(range(len(partners))):
            sent[c, n].wait_recv()
        for l in range(layers):
            value = summed[l, chunk(c)]
            for n in range(len(partners)):
                value = value + incoming[c, n, l].astype(jnp.float32)
            summed[l, chunk(c)] = value
    for l in range(layers):
        out_ref[l] = summed[l].T.reshape(out_ref.shape[1:])

    def drain(q):
        for c in range(chunks):
            for n in range(len(sends[q])):
                east(q, n, c).wait_send()

    per_parity(drain)
    for copy in sent.values():
        copy.wait_send()


def per_device(lats, lons, residual, noise_weights, kernel):
    offsets, layers, rows, cells = kernel.shape
    probes = residual.shape[2]
    band = cells // lats
    chunks = 2 if probes % 32 == 0 else 1
    part = probes // chunks
    remote = pl.BlockSpec(memory_space=pltpu.HBM)
    return pl.pallas_call(
        functools.partial(sweep, lats, lons),
        out_shape=jax.ShapeDtypeStruct(
            (layers, residual.shape[0], residual.shape[1], probes), jnp.float32
        ),
        in_specs=[remote, remote, remote],
        out_specs=pl.BlockSpec(memory_space=pltpu.VMEM),
        scratch_shapes=[
            pltpu.VMEM(residual.shape, jnp.bfloat16),
            pltpu.VMEM(noise_weights.shape[::-1], jnp.float32),
            pltpu.VMEM((offsets, layers, rows, cells), jnp.bfloat16),
            pltpu.VMEM((offsets, probes, rows), jnp.bfloat16),
            pltpu.VMEM((layers, probes, cells), jnp.float32),
            pltpu.VMEM((chunks, lats - 1, layers, part, band), jnp.bfloat16),
            pltpu.VMEM((chunks, lats - 1, layers, part, band), jnp.bfloat16),
            pltpu.VMEM((layers, probes, band), jnp.float32),
            pltpu.SemaphoreType.DMA((2,)),
            pltpu.SemaphoreType.DMA((offsets,)),
            pltpu.SemaphoreType.DMA((2 * offsets, chunks)),
            pltpu.SemaphoreType.DMA((offsets, chunks)),
            pltpu.SemaphoreType.DMA((chunks, lats - 1)),
            pltpu.SemaphoreType.DMA((chunks, lats - 1)),
        ],
        compiler_params=pltpu.CompilerParams(
            collective_id=0, has_side_effects=True, vmem_limit_bytes=63 * 1024 * 1024
        ),
        cost_estimate=pl.CostEstimate(
            flops=2 * offsets * layers * rows * cells * probes,
            bytes_accessed=2 * offsets * layers * rows * cells,
            transcendentals=0,
        ),
    )(residual, noise_weights.T, kernel)


def solution(mesh):
    return jax.shard_map(
        functools.partial(per_device, mesh.shape["lat"], mesh.shape["lon"]),
        mesh=mesh,
        in_specs=(P("lat", "lon", None), P("lat", "lon"), P(None, None, "lat", None)),
        out_specs=P(None, "lat", "lon", None),
        check_vma=False,
    )
```

time: 127 us -> 25.6 us (0.20)
  waiting for transfers between devices: 97.4 us -> 0 us
  Pallas kernels: 0 us -> 23.8 us
  between operations: 13.4 us -> 0.01 us
  matrix products: 8.22 us -> 0 us
  other arithmetic: 2.25 us -> 0 us
  starting transfers between devices: 2.22 us -> 0 us
    ppermute x3 -> x0, waiting for transfers between devices: 73.1 us -> none  [shifted(): lax.ppermute(value, axis, [(i, (i + by) % length) for i in range(length)])]
    reduce_scatter x1 -> x0, waiting for transfers between devices: 24.3 us -> none  [per_device(): lax.psum_scatter(carried, 'lat', scatter_dimension=1, tiled=True)]
    pallas_call x0 -> x1, Pallas kernels: none -> 23.8 us  [per_device(): pl.pallas_call(functools.partial(sweep, lats, lons), out_shape=jax.ShapeD...]
    dot_general x4 -> x0, matrix products: 8.22 us -> none  [contribution(): jnp.einsum('lqc,qp->lcp', kernel_slab, weighted, preferred_element_type=j...]
    ppermute x3 -> x0, starting transfers between devices: 2.21 us -> none  [shifted(): lax.ppermute(value, axis, [(i, (i + by) % length) for i in range(length)])]
    reduce_scatter x1 -> x0, local copies, waits for them, and re-layouts: 1.78 us -> none  [per_device(): lax.psum_scatter(carried, 'lat', scatter_dimension=1, tiled=True)]
  transfers between devices with their start and end apart: 4 -> 0, of which waited for: 4 -> 0; matrix products, arithmetic and copies ran while one was open for 3% -> 0% of each run, Pallas kernels for 0% -> 0%
where the time goes in v2:
time: 25.6 us; the launch traced here: 25.5 us
  Pallas kernels  23.8 us (93%)
  local copies, waits for them, and re-layouts  1.67 us (7%)
    pallas_call x1, Pallas kernels, per_device(): pl.pallas_call(functools.partial(sweep, lats, lons), out_shape=jax.ShapeD...  23.8 us
    unnamed x1, local copies, waits for them, and re-layouts  1.67 us

profile of v2, /device:TPU:1, one launch (start us, length us, event | category | flops | bytes accessed | tf_op | source)
XLA Modules:
  0.0 25.5 jit_solution(2742593516649021541)
XLA Ops:
  0.0 23.8 %shard_map.37 = f32[1,32,16,128]{3,2,1,0:T(8,128)} custom-call(bf16[32,16,128]{2,1,0:T(8,128)(2,1)} %res_hbm.1, f32[16,32]{1,0:T(8,128)} %bitcast.1, bf16[4,1,512,2048]{3,2,1,0:T(8,128)(2,1)} %panel_hbm.1), custom_call_target="tpu_custom_call" | custom-call | flops 1073741824 | bytes 8388608 | tf_op jit(solution)/shard_map/pallas_call | solution.py:205
  23.8 1.7 %copy.5 = f32[1,32,16,128]{3,2,1,0:T(8,128)} copy(f32[1,32,16,128]{3,2,1,0:T(8,128)} %shard_map.37) | data formatting | bytes 524288

commit v3 on v2

--- a/solution.py
+++ b/solution.py
@@ -23,12 +23,12 @@
 
 def sweep(
     lats, lons, res_hbm, nw_hbm, panel_hbm, out_ref,
-    res, nw, panel, blocks, total, outgoing, incoming, summed,
-    input_sem, panel_sem, east_send, east_recv, band_send, band_recv,
+    res, nw, panel, blocks, total, chip_out, chip_in, band_out, band_in, summed,
+    input_sem, panel_sem, east_send, east_recv, chip_send, chip_recv, band_send, band_recv,
 ):
     offsets, layers, rows, cells = panel_hbm.shape
     probes = res_hbm.shape[-1]
-    chunks, part = outgoing.shape[0], outgoing.shape[3]
+    chunks, part = band_out.shape[0], band_out.shape[3]
     band = cells // lats
     lat, lon = lax.axis_index("lat"), lax.axis_index("lon")
     period, source, order = route(offsets, lons)
@@ -51,8 +51,7 @@
         to = lax.rem(lat // pair + a, groups) * pair + lax.rem(lat % pair + b, pair)
         return (to, lon)
 
-    partners = [(a, b) for a in range(groups - 1, -1, -1) for b in range(pair)][: lats]
-    partners = [ab for ab in partners if ab != (0, 0)]
+    partners = [(a, 0) for a in range(1, groups)] + [(0, b) for b in range(1, pair)]
 
     sends = [[] for _ in range(period)]
     senders = [set() for _ in range(period)]
@@ -121,7 +120,16 @@
         ).wait_recv()
 
     pl.semaphore_wait(barrier, len(senders[0]) + len(partners))
-    forward(0, range(chunks))
+    forward(0, [0])
+
+    def follow(q):
+        for c in range(1, chunks):
+            for n, send in enumerate(sends[q]):
+                if send[1] == 0:
+                    east(q, n, c - 1).wait_send()
+                    east(q, n, c).start()
+
+    per_parity(follow)
 
     def accumulate(d, first):
         loads[d].wait()
@@ -156,43 +164,70 @@
             for l in range(layers)
         ]
 
-    sent = {}
+    def inner(c, b):
+        return pltpu.make_async_remote_copy(
+            src_ref=chip_out.at[c, b - 1],
+            dst_ref=chip_in.at[c, b - 1],
+            send_sem=chip_send.at[c, b - 1],
+            recv_sem=chip_recv.at[c, b - 1],
+            device_id=across(0, b),
+            device_id_type=MESH,
+        )
+
+    def outer(c, a):
+        return pltpu.make_async_remote_copy(
+            src_ref=band_out.at[c, a - 1],
+            dst_ref=band_in.at[c, a - 1],
+            send_sem=band_send.at[c, a - 1],
+            recv_sem=band_recv.at[c, a - 1],
+            device_id=across(a, 0),
+            device_id_type=MESH,
+        )
+
     for c in range(chunks):
         arrive(last, c)
-        for n, (a, b) in enumerate(partners):
-            to = across(a, b)
-            for l, value in enumerate(finish(c, to[0])):
-                outgoing[c, n, l] = value.astype(jnp.bfloat16)
-            sent[c, n] = pltpu.make_async_remote_copy(
-                src_ref=outgoing.at[c, n],
-                dst_ref=incoming.at[c, n],
-                send_sem=band_send.at[c, n],
-                recv_sem=band_recv.at[c, n],
-                device_id=to,
-                device_id_type=MESH,
-            )
-            sent[c, n].start()
-        for l, value in enumerate(finish(c, lat)):
-            summed[l, chunk(c)] = value
+        for b in range(1, pair):
+            for a in range(groups):
+                for l, value in enumerate(finish(c, across(a, b)[0])):
+                    chip_out[c, b - 1, a, l] = value.astype(jnp.bfloat16)
+            inner(c, b).start()
+        mine = [finish(c, across(a, 0)[0]) for a in range(groups)]
+        for b in range(1, pair):
+            inner(c, b).wait_recv()
+        for a in list(range(1, groups)) + [0]:
+            for l in range(layers):
+                value = mine[a][l]
+                for b in range(1, pair):
+                    value = value + chip_in[c, b - 1, a, l].astype(jnp.float32)
+                if a == 0:
+                    summed[l, chunk(c)] = value
+                else:
+                    band_out[c, a - 1, l] = value.astype(jnp.bfloat16)
+            if a > 0:
+                outer(c, a).start()
     for c in range(chunks):
-        for n in reversed(range(len(partners))):
-            sent[c, n].wait_recv()
+        for a in range(1, groups):
+            outer(c, a).wait_recv()
         for l in range(layers):
             value = summed[l, chunk(c)]
-            for n in range(len(partners)):
-                value = value + incoming[c, n, l].astype(jnp.float32)
+            for a in range(1, groups):
+                value = value + band_in[c, a - 1, l].astype(jnp.float32)
             summed[l, chunk(c)] = value
     for l in range(layers):
         out_ref[l] = summed[l].T.reshape(out_ref.shape[1:])
 
     def drain(q):
         for c in range(chunks):
-            for n in range(len(sends[q])):
-                east(q, n, c).wait_send()
+            for n, send in enumerate(sends[q]):
+                if send[1] > 0 or c == chunks - 1:
+                    east(q, n, c).wait_send()
 
     per_parity(drain)
-    for copy in sent.values():
-        copy.wait_send()
+    for c in range(chunks):
+        for b in range(1, pair):
+            inner(c, b).wait_send()
+        for a in range(1, groups):
+            outer(c, a).wait_send()
 
 
 def per_device(lats, lons, residual, noise_weights, kernel):
@@ -201,6 +236,9 @@
     band = cells // lats
     chunks = 2 if probes % 32 == 0 else 1
     part = probes // chunks
+    pair = 2 if lats % 2 == 0 else 1
+    groups = lats // pair
+    inner, outer = max(pair - 1, 1), max(groups - 1, 1)
     remote = pl.BlockSpec(memory_space=pltpu.HBM)
     return pl.pallas_call(
         functools.partial(sweep, lats, lons),
@@ -215,15 +253,19 @@
             pltpu.VMEM((offsets, layers, rows, cells), jnp.bfloat16),
             pltpu.VMEM((offsets, probes, rows), jnp.bfloat16),
             pltpu.VMEM((layers, probes, cells), jnp.float32),
-            pltpu.VMEM((chunks, lats - 1, layers, part, band), jnp.bfloat16),
-            pltpu.VMEM((chunks, lats - 1, layers, part, band), jnp.bfloat16),
+            pltpu.VMEM((chunks, inner, groups, layers, part, band), jnp.bfloat16),
+            pltpu.VMEM((chunks, inner, groups, layers, part, band), jnp.bfloat16),
+            pltpu.VMEM((chunks, outer, layers, part, band), jnp.bfloat16),
+            pltpu.VMEM((chunks, outer, layers, part, band), jnp.bfloat16),
             pltpu.VMEM((layers, probes, band), jnp.float32),
             pltpu.SemaphoreType.DMA((2,)),
             pltpu.SemaphoreType.DMA((offsets,)),
             pltpu.SemaphoreType.DMA((2 * offsets, chunks)),
             pltpu.SemaphoreType.DMA((offsets, chunks)),
-            pltpu.SemaphoreType.DMA((chunks, lats - 1)),
-            pltpu.SemaphoreType.DMA((chunks, lats - 1)),
+            pltpu.SemaphoreType.DMA((chunks, inner)),
+            pltpu.SemaphoreType.DMA((chunks, inner)),
+            pltpu.SemaphoreType.DMA((chunks, outer)),
+            pltpu.SemaphoreType.DMA((chunks, outer)),
         ],
         compiler_params=pltpu.CompilerParams(
             collective_id=0, has_side_effects=True, vmem_limit_bytes=63 * 1024 * 1024

time: 25.6 us -> 27.1 us (1.059)
  the two profiles are of different devices: /device:TPU:1 before, /device:TPU:0 now
where the time goes in v3:
time: 27.1 us; the launch traced here: 26.9 us
  Pallas kernels  25.3 us (93%)
  local copies, waits for them, and re-layouts  1.67 us (6%)
    pallas_call x1, Pallas kernels, per_device(): pl.pallas_call(functools.partial(sweep, lats, lons), out_shape=jax.ShapeD...  25.3 us
    unnamed x1, local copies, waits for them, and re-layouts  1.67 us

profile of v3, /device:TPU:0, one launch (start us, length us, event | category | flops | bytes accessed | tf_op | source)
XLA Modules:
  0.0 26.9 jit_solution(13679381531914366793)
XLA Ops:
  0.0 25.3 %shard_map.37 = f32[1,32,16,128]{3,2,1,0:T(8,128)} custom-call(bf16[32,16,128]{2,1,0:T(8,128)(2,1)} %res_hbm.1, f32[16,32]{1,0:T(8,128)} %bitcast.1, bf16[4,1,512,2048]{3,2,1,0:T(8,128)(2,1)} %panel_hbm.1), custom_call_target="tpu_custom_call" | custom-call | flops 1073741824 | bytes 8388608 | tf_op jit(solution)/shard_map/pallas_call | solution.py:243
  25.3 1.7 %copy.5 = f32[1,32,16,128]{3,2,1,0:T(8,128)} copy(f32[1,32,16,128]{3,2,1,0:T(8,128)} %shard_map.37) | data formatting | bytes 524288

commit v4 on v2

v4 whole, which is shorter than its diff:
```python
import functools

import jax
import jax.numpy as jnp
from jax import lax
from jax.experimental import pallas as pl
from jax.experimental.pallas import tpu as pltpu
from jax.sharding import PartitionSpec as P

MESH = pl.DeviceIdType.MESH


def route(offsets, lons):
    if lons % 2 or offsets < 3:
        table = {d: (-d, 0) for d in range(1, offsets)}
        return 1, [table], list(range(1, offsets))
    even, odd = {}, {}
    for d in range(1, offsets):
        even[d] = (1, 2) if d == 1 else (-2, d - 2)
        odd[d] = (-1, d - 1) if d % 2 else (-2, d - 2)
    return 2, [even, odd], list(range(2, offsets, 2)) + list(range(1, offsets, 2))


def sweep(
    lats, lons, res_hbm, nw_hbm, panel_hbm, out_ref,
    res, nw, panel, blocks, total, chip_out, chip_in, band_out, band_in,
    input_sem, panel_sem, east_send, east_recv, chip_send, chip_recv, band_send, band_recv,
):
    offsets, layers, rows, cells = panel_hbm.shape
    probes = res_hbm.shape[-1]
    chunks, part = blocks.shape[1], blocks.shape[3]
    band = cells // lats
    lat, lon = lax.axis_index("lat"), lax.axis_index("lon")
    period, source, order = route(offsets, lons)
    pair = 2 if lats % 2 == 0 else 1
    groups = lats // pair

    res_load = pltpu.make_async_copy(res_hbm, res, input_sem.at[0])
    nw_load = pltpu.make_async_copy(nw_hbm, nw, input_sem.at[1])
    res_load.start()
    nw_load.start()
    loads = {}
    for d in [0] + order:
        loads[d] = pltpu.make_async_copy(panel_hbm.at[d], panel.at[d], panel_sem.at[d])
        loads[d].start()

    def along(delta):
        return (lat, lax.rem(lon + (delta + lons), lons))

    def across(a, b):
        to = lax.rem(lat // pair + a, groups) * pair + lax.rem(lat % pair + b, pair)
        return (to, lon)

    partners = [(a, 0) for a in range(1, groups)] + [(0, b) for b in range(1, pair)]

    sends = [[] for _ in range(period)]
    senders = [set() for _ in range(period)]
    for q in range(period):
        for d in order:
            delta, held = source[q][d]
            sends[(q + delta) % period].append((-delta, held, d))
            senders[q].add(delta)

    def per_parity(action):
        for q in range(period):
            if period == 1:
                action(q)
            else:
                pl.when(lax.rem(lon, period) == q)(functools.partial(action, q))

    barrier = pltpu.get_barrier_semaphore()

    def greet(q):
        for delta in sorted(senders[q]):
            pl.semaphore_signal(barrier, inc=1, device_id=along(delta), device_id_type=MESH)

    per_parity(greet)
    for a, b in partners:
        pl.semaphore_signal(barrier, inc=1, device_id=across(a, b), device_id_type=MESH)

    res_load.wait()
    nw_load.wait()
    columns = res.shape[1]
    pieces = [
        nw[:, y : y + 1] * res[y].astype(jnp.float32) for y in range(rows // columns)
    ]
    weighted = jnp.concatenate(pieces, axis=0).T.astype(jnp.bfloat16)
    for c in range(chunks):
        blocks[0, c] = weighted[:, c * part : (c + 1) * part]

    def east(q, n, c):
        delta, held, d = sends[q][n]
        return pltpu.make_async_remote_copy(
            src_ref=blocks.at[held, c],
            dst_ref=blocks.at[d, c],
            send_sem=east_send.at[n, c],
            recv_sem=east_recv.at[d, c],
            device_id=along(delta),
            device_id_type=MESH,
        )

    def forward(held, cs):
        def action(q):
            for c in cs:
                for n, send in enumerate(sends[q]):
                    if send[1] == held:
                        east(q, n, c).start()

        per_parity(action)

    def arrive(d, c):
        pltpu.make_async_remote_copy(
            src_ref=blocks.at[d, c],
            dst_ref=blocks.at[d, c],
            send_sem=east_send.at[0, c],
            recv_sem=east_recv.at[d, c],
            device_id=along(1),
            device_id_type=MESH,
        ).wait_recv()

    pl.semaphore_wait(barrier, len(senders[0]) + len(partners))
    forward(0, range(chunks))

    def product(d, c, l, cols):
        return jnp.dot(
            blocks[d, c], panel[d, l, pl.ds(c * part, part), cols],
            preferred_element_type=jnp.float32,
        )

    def accumulate(d, cs, first):
        for l in range(layers):

            @pl.loop(0, lats)
            def _(b):
                cols = pl.ds(pl.multiple_of(b * band, band), band)
                value = None if first else total[l, :, cols]
                for c in cs:
                    more = product(d, c, l, cols)
                    value = more if value is None else value + more
                total[l, :, cols] = value

    loads[0].wait()
    accumulate(0, range(chunks), True)
    for d in order[:-1]:
        for c in range(chunks):
            arrive(d, c)
            forward(d, [c])
        loads[d].wait()
        accumulate(d, range(chunks), False)

    last = order[-1]
    loads[last].wait()
    for c in range(chunks - 1):
        arrive(last, c)
        accumulate(last, [c], False)
    arrive(last, chunks - 1)

    def finish(to):
        cols = pl.ds(pl.multiple_of(to * band, band), band)
        return [
            total[l, :, cols] + product(last, chunks - 1, l, cols) for l in range(layers)
        ]

    def inner(a, b):
        return pltpu.make_async_remote_copy(
            src_ref=chip_out.at[a, b - 1],
            dst_ref=chip_in.at[a, b - 1],
            send_sem=chip_send.at[a, b - 1],
            recv_sem=chip_recv.at[a, b - 1],
            device_id=across(0, b),
            device_id_type=MESH,
        )

    def outer(a):
        return pltpu.make_async_remote_copy(
            src_ref=band_out.at[a - 1],
            dst_ref=band_in.at[a - 1],
            send_sem=band_send.at[a - 1],
            recv_sem=band_recv.at[a - 1],
            device_id=across(a, 0),
            device_id_type=MESH,
        )

    def offer(a):
        for b in range(1, pair):
            for l, value in enumerate(finish(across(a, b)[0])):
                chip_out[a, b - 1, l] = value.astype(jnp.bfloat16)
            inner(a, b).start()

    def collect(a, values):
        for b in range(1, pair):
            inner(a, b).wait_recv()
            values = [
                value + chip_in[a, b - 1, l].astype(jnp.float32)
                for l, value in enumerate(values)
            ]
        return values

    steps = list(range(1, groups)) + [0]
    offer(steps[0])
    for n, a in enumerate(steps):
        mine = finish(across(a, 0)[0])
        if n + 1 < groups:
            offer(steps[n + 1])
        mine = collect(a, mine)
        if a > 0:
            for l, value in enumerate(mine):
                band_out[a - 1, l] = value.astype(jnp.bfloat16)
            outer(a).start()
    for a in range(1, groups):
        outer(a).wait_recv()
        mine = [
            value + band_in[a - 1, l].astype(jnp.float32) for l, value in enumerate(mine)
        ]
    for l, value in enumerate(mine):
        out_ref[l] = value.T.reshape(out_ref.shape[1:])

    def drain(q):
        for c in range(chunks):
            for n in range(len(sends[q])):
                east(q, n, c).wait_send()

    per_parity(drain)
    for a in range(groups):
        for b in range(1, pair):
            inner(a, b).wait_send()
        if a > 0:
            outer(a).wait_send()


def per_device(lats, lons, residual, noise_weights, kernel):
    offsets, layers, rows, cells = kernel.shape
    probes = residual.shape[2]
    band = cells // lats
    chunks = 2 if rows % 256 == 0 else 1
    pair = 2 if lats % 2 == 0 else 1
    groups = lats // pair
    inner, outer = max(pair - 1, 1), max(groups - 1, 1)
    remote = pl.BlockSpec(memory_space=pltpu.HBM)
    return pl.pallas_call(
        functools.partial(sweep, lats, lons),
        out_shape=jax.ShapeDtypeStruct(
            (layers, residual.shape[0], residual.shape[1], probes), jnp.float32
        ),
        in_specs=[remote, remote, remote],
        out_specs=pl.BlockSpec(memory_space=pltpu.VMEM),
        scratch_shapes=[
            pltpu.VMEM(residual.shape, jnp.bfloat16),
            pltpu.VMEM(noise_weights.shape[::-1], jnp.float32),
            pltpu.VMEM((offsets, layers, rows, cells), jnp.bfloat16),
            pltpu.VMEM((offsets, chunks, probes, rows // chunks), jnp.bfloat16),
            pltpu.VMEM((layers, probes, cells), jnp.float32),
            pltpu.VMEM((groups, inner, layers, probes, band), jnp.bfloat16),
            pltpu.VMEM((groups, inner, layers, probes, band), jnp.bfloat16),
            pltpu.VMEM((outer, layers, probes, band), jnp.bfloat16),
            pltpu.VMEM((outer, layers, probes, band), jnp.bfloat16),
            pltpu.SemaphoreType.DMA((2,)),
            pltpu.SemaphoreType.DMA((offsets,)),
            pltpu.SemaphoreType.DMA((2 * offsets, chunks)),
            pltpu.SemaphoreType.DMA((offsets, chunks)),
            pltpu.SemaphoreType.DMA((groups, inner)),
            pltpu.SemaphoreType.DMA((groups, inner)),
            pltpu.SemaphoreType.DMA((outer,)),
            pltpu.SemaphoreType.DMA((outer,)),
        ],
        compiler_params=pltpu.CompilerParams(
            collective_id=0, has_side_effects=True, vmem_limit_bytes=63 * 1024 * 1024
        ),
        cost_estimate=pl.CostEstimate(
            flops=2 * offsets * layers * rows * cells * probes,
            bytes_accessed=2 * offsets * layers * rows * cells,
            transcendentals=0,
        ),
    )(residual, noise_weights.T, kernel)


def solution(mesh):
    return jax.shard_map(
        functools.partial(per_device, mesh.shape["lat"], mesh.shape["lon"]),
        mesh=mesh,
        in_specs=(P("lat", "lon", None), P("lat", "lon"), P(None, None, "lat", None)),
        out_specs=P(None, "lat", "lon", None),
        check_vma=False,
    )
```

time: 25.6 us -> 26.9 us (1.051); the launches traced: 25.5 us -> 26.5 us
  Pallas kernels: 23.8 us -> 24.8 us
    pallas_call x1, Pallas kernels: 23.8 us -> 24.8 us  [per_device(): pl.pallas_call(functools.partial(sweep, lats, lons), out_shape=jax.ShapeD...]
where the time goes in v4:
time: 26.9 us; the launch traced here: 26.5 us
  Pallas kernels  24.8 us (92%)
  local copies, waits for them, and re-layouts  1.67 us (6%)
    pallas_call x1, Pallas kernels, per_device(): pl.pallas_call(functools.partial(sweep, lats, lons), out_shape=jax.ShapeD...  24.8 us
    unnamed x1, local copies, waits for them, and re-layouts  1.67 us

profile of v4, /device:TPU:1, one launch (start us, length us, event | category | flops | bytes accessed | tf_op | source)
XLA Modules:
  0.0 26.5 jit_solution(6422131649073909497)
XLA Ops:
  0.0 24.8 %shard_map.37 = f32[1,32,16,128]{3,2,1,0:T(8,128)} custom-call(bf16[32,16,128]{2,1,0:T(8,128)(2,1)} %res_hbm.1, f32[16,32]{1,0:T(8,128)} %bitcast.1, bf16[4,1,512,2048]{3,2,1,0:T(8,128)(2,1)} %panel_hbm.1), custom_call_target="tpu_custom_call" | custom-call | flops 1073741824 | bytes 8388608 | tf_op jit(solution)/shard_map/pallas_call | solution.py:240
  24.8 1.7 %copy.5 = f32[1,32,16,128]{3,2,1,0:T(8,128)} copy(f32[1,32,16,128]{3,2,1,0:T(8,128)} %shard_map.37) | data formatting | bytes 524288

commit v5 on v2

--- a/solution.py
+++ b/solution.py
@@ -10,15 +10,21 @@
 MESH = pl.DeviceIdType.MESH
 
 
-def route(offsets, lons):
-    if lons % 2 or offsets < 3:
-        table = {d: (-d, 0) for d in range(1, offsets)}
-        return 1, [table], list(range(1, offsets))
-    even, odd = {}, {}
-    for d in range(1, offsets):
-        even[d] = (1, 2) if d == 1 else (-2, d - 2)
-        odd[d] = (-1, d - 1) if d % 2 else (-2, d - 2)
-    return 2, [even, odd], list(range(2, offsets, 2)) + list(range(1, offsets, 2))
+def route(offsets, lons, chunks):
+    direct = {d: (-d, 0) for d in range(1, offsets)}
+    if lons % 2 or offsets < 3 or lons <= offsets:
+        return 1, [[direct] * chunks], list(range(1, offsets))
+    even, odd = [], []
+    for c in range(chunks):
+        even.append({**direct, 1: (1, 2)})
+        odd.append(dict(direct))
+        if offsets > 3:
+            odd[c][3] = (-1, 2)
+            if c % 2:
+                even[c][3] = (1, offsets)
+                odd[c][offsets] = (-4, 0)
+    rest = [d for d in range(1, offsets) if d != 2]
+    return 2, [even, odd], [2, offsets] + rest
 
 
 def sweep(
@@ -31,7 +37,7 @@
     chunks, part = outgoing.shape[0], outgoing.shape[3]
     band = cells // lats
     lat, lon = lax.axis_index("lat"), lax.axis_index("lon")
-    period, source, order = route(offsets, lons)
+    period, source, order = route(offsets, lons, chunks)
     pair = 2 if lats % 2 == 0 else 1
     groups = lats // pair
 
@@ -40,7 +46,7 @@
     res_load.start()
     nw_load.start()
     loads = {}
-    for d in [0] + order:
+    for d in [0] + [d for d in order if d < offsets]:
         loads[d] = pltpu.make_async_copy(panel_hbm.at[d], panel.at[d], panel_sem.at[d])
         loads[d].start()
 
@@ -54,13 +60,19 @@
     partners = [(a, b) for a in range(groups - 1, -1, -1) for b in range(pair)][: lats]
     partners = [ab for ab in partners if ab != (0, 0)]
 
-    sends = [[] for _ in range(period)]
+    sends = [[[] for _ in range(chunks)] for _ in range(period)]
     senders = [set() for _ in range(period)]
     for q in range(period):
-        for d in order:
-            delta, held = source[q][d]
-            sends[(q + delta) % period].append((-delta, held, d))
-            senders[q].add(delta)
+        for c in range(chunks):
+            for d in order:
+                if d in source[q][c]:
+                    delta, held = source[q][c][d]
+                    sends[(q + delta) % period][c].append((-delta, held, d))
+                    senders[q].add(delta)
+    for lists in sends:
+        for some in lists:
+            some.sort(key=lambda send: order.index(send[2]))
+    receivers = [{send[0] for c in range(chunks) for send in sends[q][c]} for q in range(period)]
 
     def per_parity(action):
         for q in range(period):
@@ -91,7 +103,7 @@
         return pl.ds(c * part, part)
 
     def east(q, n, c):
-        delta, held, d = sends[q][n]
+        delta, held, d = sends[q][c][n]
         return pltpu.make_async_remote_copy(
             src_ref=blocks.at[held, chunk(c)],
             dst_ref=blocks.at[d, chunk(c)],
@@ -101,12 +113,25 @@
             device_id_type=MESH,
         )
 
-    def forward(held, cs):
+    def outgoing_of(q, held, c):
+        return [n for n, send in enumerate(sends[q][c]) if send[1] == held]
+
+    def forward(held, c):
         def action(q):
-            for c in cs:
-                for n, send in enumerate(sends[q]):
-                    if send[1] == held:
-                        east(q, n, c).start()
+            for n in outgoing_of(q, held, c):
+                east(q, n, c).start()
+
+        per_parity(action)
+
+    def follow(c):
+        def action(q):
+            before, now = outgoing_of(q, 0, c - 1), outgoing_of(q, 0, c)
+            for n in before:
+                east(q, n, c - 1).wait_send()
+                if now:
+                    east(q, now.pop(0), c).start()
+            for n in now:
+                east(q, n, c).start()
 
         per_parity(action)
 
@@ -120,8 +145,13 @@
             device_id_type=MESH,
         ).wait_recv()
 
-    pl.semaphore_wait(barrier, len(senders[0]) + len(partners))
-    forward(0, range(chunks))
+    def admit(q):
+        pl.semaphore_wait(barrier, len(receivers[q]) + len(partners))
+
+    per_parity(admit)
+    forward(0, 0)
+    for c in range(1, chunks):
+        follow(c)
 
     def accumulate(d, first):
         loads[d].wait()
@@ -136,11 +166,22 @@
                 total[l, :, cols] = value if first else total[l, :, cols] + value
 
     accumulate(0, True)
-    for d in order[:-1]:
-        for c in range(chunks):
-            arrive(d, c)
-            forward(d, [c])
-        accumulate(d, False)
+    def relay(d):
+        def action(q):
+            for c in range(chunks):
+                if d in source[q][c]:
+                    arrive(d, c)
+                    for n in outgoing_of(q, d, c):
+                        east(q, n, c).start()
+
+        per_parity(action)
+
+    for n, d in enumerate(order[:-1]):
+        relay(d)
+        if d == offsets:
+            accumulate(order[n - 1], False)
+        elif order[n + 1] != offsets:
+            accumulate(d, False)
 
     last = order[-1]
     loads[last].wait()
@@ -187,8 +228,9 @@
 
     def drain(q):
         for c in range(chunks):
-            for n in range(len(sends[q])):
-                east(q, n, c).wait_send()
+            for n, send in enumerate(sends[q][c]):
+                if send[1] > 0 or c == chunks - 1:
+                    east(q, n, c).wait_send()
 
     per_parity(drain)
     for copy in sent.values():
@@ -213,7 +255,7 @@
             pltpu.VMEM(residual.shape, jnp.bfloat16),
             pltpu.VMEM(noise_weights.shape[::-1], jnp.float32),
             pltpu.VMEM((offsets, layers, rows, cells), jnp.bfloat16),
-            pltpu.VMEM((offsets, probes, rows), jnp.bfloat16),
+            pltpu.VMEM((offsets + 1, probes, rows), jnp.bfloat16),
             pltpu.VMEM((layers, probes, cells), jnp.float32),
             pltpu.VMEM((chunks, lats - 1, layers, part, band), jnp.bfloat16),
             pltpu.VMEM((chunks, lats - 1, layers, part, band), jnp.bfloat16),
@@ -221,7 +263,7 @@
             pltpu.SemaphoreType.DMA((2,)),
             pltpu.SemaphoreType.DMA((offsets,)),
             pltpu.SemaphoreType.DMA((2 * offsets, chunks)),
-            pltpu.SemaphoreType.DMA((offsets, chunks)),
+            pltpu.SemaphoreType.DMA((offsets + 1, chunks)),
             pltpu.SemaphoreType.DMA((chunks, lats - 1)),
             pltpu.SemaphoreType.DMA((chunks, lats - 1)),
         ],

time: 25.6 us -> 27.8 us (1.086)
  Pallas kernels: 23.8 us -> 26 us
    pallas_call x1, Pallas kernels: 23.8 us -> 26 us  [per_device(): pl.pallas_call(functools.partial(sweep, lats, lons), out_shape=jax.ShapeD...]
where the time goes in v5:
time: 27.8 us; the launch traced here: 27.7 us
  Pallas kernels  26 us (94%)
  local copies, waits for them, and re-layouts  1.67 us (6%)
    pallas_call x1, Pallas kernels, per_device(): pl.pallas_call(functools.partial(sweep, lats, lons), out_shape=jax.ShapeD...  26 us
    unnamed x1, local copies, waits for them, and re-layouts  1.67 us

profile of v5, /device:TPU:1, one launch (start us, length us, event | category | flops | bytes accessed | tf_op | source)
XLA Modules:
  0.0 27.7 jit_solution(15509520114187209322)
XLA Ops:
  0.0 26.0 %shard_map.37 = f32[1,32,16,128]{3,2,1,0:T(8,128)} custom-call(bf16[32,16,128]{2,1,0:T(8,128)(2,1)} %res_hbm.1, f32[16,32]{1,0:T(8,128)} %bitcast.1, bf16[4,1,512,2048]{3,2,1,0:T(8,128)(2,1)} %panel_hbm.1), custom_call_target="tpu_custom_call" | custom-call | flops 1073741824 | bytes 8388608 | tf_op jit(solution)/shard_map/pallas_call | solution.py:247
  26.0 1.7 %copy.5 = f32[1,32,16,128]{3,2,1,0:T(8,128)} copy(f32[1,32,16,128]{3,2,1,0:T(8,128)} %shard_map.37) | data formatting | bytes 524288

commit v6 on v5

--- a/solution.py
+++ b/solution.py
@@ -21,8 +21,11 @@
         if offsets > 3:
             odd[c][3] = (-1, 2)
             if c % 2:
+                even[c][offsets] = (1, 0)
+                even[c][3] = (-4, offsets)
+            else:
+                odd[c][offsets] = (-4, 0)
                 even[c][3] = (1, offsets)
-                odd[c][offsets] = (-4, 0)
     rest = [d for d in range(1, offsets) if d != 2]
     return 2, [even, odd], [2, offsets] + rest
 
@@ -123,18 +126,6 @@
 
         per_parity(action)
 
-    def follow(c):
-        def action(q):
-            before, now = outgoing_of(q, 0, c - 1), outgoing_of(q, 0, c)
-            for n in before:
-                east(q, n, c - 1).wait_send()
-                if now:
-                    east(q, now.pop(0), c).start()
-            for n in now:
-                east(q, n, c).start()
-
-        per_parity(action)
-
     def arrive(d, c):
         pltpu.make_async_remote_copy(
             src_ref=blocks.at[d, chunk(c)],
@@ -149,9 +140,8 @@
         pl.semaphore_wait(barrier, len(receivers[q]) + len(partners))
 
     per_parity(admit)
-    forward(0, 0)
-    for c in range(1, chunks):
-        follow(c)
+    for c in range(chunks):
+        forward(0, c)
 
     def accumulate(d, first):
         loads[d].wait()
@@ -228,9 +218,8 @@
 
     def drain(q):
         for c in range(chunks):
-            for n, send in enumerate(sends[q][c]):
-                if send[1] > 0 or c == chunks - 1:
-                    east(q, n, c).wait_send()
+            for n in range(len(sends[q][c])):
+                east(q, n, c).wait_send()
 
     per_parity(drain)
     for copy in sent.values():
@@ -268,7 +257,7 @@
             pltpu.SemaphoreType.DMA((chunks, lats - 1)),
         ],
         compiler_params=pltpu.CompilerParams(
-            collective_id=0, has_side_effects=True, vmem_limit_bytes=63 * 1024 * 1024
+            collective_id=0, has_side_effects=True, vmem_limit_bytes=48 * 1024 * 1024
         ),
         cost_estimate=pl.CostEstimate(
             flops=2 * offsets * layers * rows * cells * probes,

time: 27.8 us -> 25.4 us (0.914)
  Pallas kernels: 26 us -> 22.9 us
  local copies, waits for them, and re-layouts: 1.67 us -> 2.31 us
    pallas_call x1, Pallas kernels: 26 us -> 22.9 us  [per_device(): pl.pallas_call(functools.partial(sweep, lats, lons), out_shape=jax.ShapeD...]
    unnamed x1 -> x5, local copies, waits for them, and re-layouts: 1.67 us -> 2.31 us
where the time goes in v6:
time: 25.4 us; the launch traced here: 25.2 us
  Pallas kernels  22.9 us (90%)
  local copies, waits for them, and re-layouts  2.31 us (9%)
    pallas_call x1, Pallas kernels, per_device(): pl.pallas_call(functools.partial(sweep, lats, lons), out_shape=jax.ShapeD...  22.9 us
    unnamed x5, local copies, waits for them, and re-layouts  2.31 us

profile of v6, /device:TPU:1, one launch (start us, length us, event | category | flops | bytes accessed | tf_op | source)
XLA Modules:
  0.0 25.2 jit_solution(5888805923092777944)
XLA Ops:
  0.0 0.0 copy-start
  0.0 0.9 %copy-done = bf16[32,16,128]{2,1,0:T(8,128)(2,1)S(1)} copy-done((bf16[32,16,128]{2,1,0:T(8,128)(2,1)S(1)}, bf16[32,16,128]{2,1,0:T(8,128)(2,1)}, u32[]{:S(2)}) %copy-start) | copy-done | bytes 131096
  0.9 0.0 copy-start.1
  0.9 0.7 %copy-done.1 = f32[32,16]{0,1:T(8,128)S(1)} copy-done((f32[32,16]{0,1:T(8,128)S(1)}, f32[32,16]{0,1:T(8,128)}, u32[]{:S(2)}) %copy-start.1) | copy-done | bytes 2072
  1.6 22.9 %shard_map.37 = f32[1,32,16,128]{3,2,1,0:T(8,128)S(1)} custom-call(bf16[32,16,128]{2,1,0:T(8,128)(2,1)S(1)} %copy-done, f32[16,32]{1,0:T(8,128)S(1)} %bitcast.1, bf16[4,1,512,2048]{3,2,1,0:T(8,128)(2,1)} %panel_hbm.1), custom_call_target="tpu_custom_call" | custom-call | flops 1073741824 | bytes 8388608 | tf_op jit(solution)/shard_map/pallas_call | solution.py:236
  24.5 0.7 %copy.5 = f32[1,32,16,128]{3,2,1,0:T(8,128)} copy(f32[1,32,16,128]{3,2,1,0:T(8,128)S(1)} %shard_map.37) | data formatting | bytes 524288
Async XLA Ops:
  0.0 0.9 %copy-start = (bf16[32,16,128]{2,1,0:T(8,128)(2,1)S(1)}, bf16[32,16,128]{2,1,0:T(8,128)(2,1)}, u32[]{:S(2)}) copy-start(bf16[32,16,128]{2,1,0:T(8,128)(2,1)} %res_hbm.1) | copy-start | bytes 393220
  0.9 0.7 %copy-start.1 = (f32[32,16]{0,1:T(8,128)S(1)}, f32[32,16]{0,1:T(8,128)}, u32[]{:S(2)}) copy-start(f32[32,16]{0,1:T(8,128)} %param.4) | copy-start | bytes 6148

commit v7 on v6

--- a/solution.py
+++ b/solution.py
@@ -176,43 +176,48 @@
     last = order[-1]
     loads[last].wait()
 
-    def finish(c, to):
-        cols = pl.ds(pl.multiple_of(to * band, band), band)
-        return [
-            total[l, chunk(c), cols]
-            + jnp.dot(
-                blocks[last, chunk(c)], panel[last, l, :, cols],
-                preferred_element_type=jnp.float32,
-            )
-            for l in range(layers)
-        ]
-
-    sent = {}
-    for c in range(chunks):
+    def band_copy(c, n):
+        return pltpu.make_async_remote_copy(
+            src_ref=outgoing.at[c, n],
+            dst_ref=incoming.at[c, n],
+            send_sem=band_send.at[c, n],
+            recv_sem=band_recv.at[c, n],
+            device_id=across(groups - 1 - n // pair, pair - 1 - n % pair),
+            device_id_type=MESH,
+        )
+
+    @pl.loop(0, chunks)
+    def _(c):
         arrive(last, c)
-        for n, (a, b) in enumerate(partners):
-            to = across(a, b)
-            for l, value in enumerate(finish(c, to[0])):
+        here = pl.ds(pl.multiple_of(c * part, part), part)
+
+        @pl.loop(0, lats)
+        def _(n):
+            to = across(groups - 1 - n // pair, pair - 1 - n % pair)[0]
+            cols = pl.ds(pl.multiple_of(to * band, band), band)
+            for l in range(layers):
+                value = total[l, here, cols] + jnp.dot(
+                    blocks[last, here], panel[last, l, :, cols],
+                    preferred_element_type=jnp.float32,
+                )
                 outgoing[c, n, l] = value.astype(jnp.bfloat16)
-            sent[c, n] = pltpu.make_async_remote_copy(
-                src_ref=outgoing.at[c, n],
-                dst_ref=incoming.at[c, n],
-                send_sem=band_send.at[c, n],
-                recv_sem=band_recv.at[c, n],
-                device_id=to,
-                device_id_type=MESH,
-            )
-            sent[c, n].start()
-        for l, value in enumerate(finish(c, lat)):
-            summed[l, chunk(c)] = value
-    for c in range(chunks):
-        for n in reversed(range(len(partners))):
-            sent[c, n].wait_recv()
+                summed[l, here] = value
+
+            @pl.when(n < lats - 1)
+            def _():
+                band_copy(c, n).start()
+
+    @pl.loop(0, chunks)
+    def _(c):
+        here = pl.ds(pl.multiple_of(c * part, part), part)
+        for n in range(lats - 1):
+            band_copy(c, n).wait_recv()
         for l in range(layers):
-            value = summed[l, chunk(c)]
-            for n in range(len(partners)):
+            value = summed[l, here]
+            for n in range(lats - 1):
                 value = value + incoming[c, n, l].astype(jnp.float32)
-            summed[l, chunk(c)] = value
+            summed[l, here] = value
+
     for l in range(layers):
         out_ref[l] = summed[l].T.reshape(out_ref.shape[1:])
 
@@ -222,8 +227,12 @@
                 east(q, n, c).wait_send()
 
     per_parity(drain)
-    for copy in sent.values():
-        copy.wait_send()
+
+    @pl.loop(0, chunks)
+    def _(c):
+        @pl.loop(0, lats - 1)
+        def _(n):
+            band_copy(c, n).wait_send()
 
 
 def per_device(lats, lons, residual, noise_weights, kernel):
@@ -246,7 +255,7 @@
             pltpu.VMEM((offsets, layers, rows, cells), jnp.bfloat16),
             pltpu.VMEM((offsets + 1, probes, rows), jnp.bfloat16),
             pltpu.VMEM((layers, probes, cells), jnp.float32),
-            pltpu.VMEM((chunks, lats - 1, layers, part, band), jnp.bfloat16),
+            pltpu.VMEM((chunks, lats, layers, part, band), jnp.bfloat16),
             pltpu.VMEM((chunks, lats - 1, layers, part, band), jnp.bfloat16),
             pltpu.VMEM((layers, probes, band), jnp.float32),
             pltpu.SemaphoreType.DMA((2,)),
@@ -257,7 +266,7 @@
             pltpu.SemaphoreType.DMA((chunks, lats - 1)),
         ],
         compiler_params=pltpu.CompilerParams(
-            collective_id=0, has_side_effects=True, vmem_limit_bytes=48 * 1024 * 1024
+            collective_id=0, has_side_effects=True, vmem_limit_bytes=63 * 1024 * 1024
         ),
         cost_estimate=pl.CostEstimate(
             flops=2 * offsets * layers * rows * cells * probes,

time: 25.4 us -> 27.6 us (1.087)
  the two profiles are of different devices: /device:TPU:1 before, /device:TPU:0 now
where the time goes in v7:
time: 27.6 us; the launch traced here: 27.4 us
  Pallas kernels  25.7 us (93%)
  local copies, waits for them, and re-layouts  1.67 us (6%)
    pallas_call x1, Pallas kernels, per_device(): pl.pallas_call(functools.partial(sweep, lats, lons), out_shape=jax.ShapeD...  25.7 us
    unnamed x1, local copies, waits for them, and re-layouts  1.67 us

profile of v7, /device:TPU:0, one launch (start us, length us, event | category | flops | bytes accessed | tf_op | source)
XLA Modules:
  0.0 27.4 jit_solution(1480661362776449821)
XLA Ops:
  0.0 25.7 %shard_map.37 = f32[1,32,16,128]{3,2,1,0:T(8,128)} custom-call(bf16[32,16,128]{2,1,0:T(8,128)(2,1)} %res_hbm.1, f32[16,32]{1,0:T(8,128)} %bitcast.1, bf16[4,1,512,2048]{3,2,1,0:T(8,128)(2,1)} %panel_hbm.1), custom_call_target="tpu_custom_call" | custom-call | flops 1073741824 | bytes 8388608 | tf_op jit(solution)/shard_map/pallas_call | solution.py:245
  25.8 1.7 %copy.5 = f32[1,32,16,128]{3,2,1,0:T(8,128)} copy(f32[1,32,16,128]{3,2,1,0:T(8,128)} %shard_map.37) | data formatting | bytes 524288

commit v8 on v6

--- a/solution.py
+++ b/solution.py
@@ -140,22 +140,34 @@
         pl.semaphore_wait(barrier, len(receivers[q]) + len(partners))
 
     per_parity(admit)
-    for c in range(chunks):
-        forward(0, c)
+    forward(0, 0)
 
     def accumulate(d, first):
         loads[d].wait()
         for l in range(layers):
-
-            @pl.loop(0, lats)
-            def _(b):
-                cols = pl.ds(pl.multiple_of(b * band, band), band)
+            for b in range(lats):
+                cols = pl.ds(b * band, band)
                 value = jnp.dot(
                     blocks[d], panel[d, l, :, cols], preferred_element_type=jnp.float32
                 )
                 total[l, :, cols] = value if first else total[l, :, cols] + value
 
     accumulate(0, True)
+
+    def follow(c):
+        def action(q):
+            before, now = outgoing_of(q, 0, c - 1), outgoing_of(q, 0, c)
+            for n in before:
+                east(q, n, c - 1).wait_send()
+                if now:
+                    east(q, now.pop(0), c).start()
+            for n in now:
+                east(q, n, c).start()
+
+        per_parity(action)
+
+    for c in range(1, chunks):
+        follow(c)
     def relay(d):
         def action(q):
             for c in range(chunks):
@@ -218,8 +230,9 @@
 
     def drain(q):
         for c in range(chunks):
-            for n in range(len(sends[q][c])):
-                east(q, n, c).wait_send()
+            for n, send in enumerate(sends[q][c]):
+                if send[1] > 0 or c == chunks - 1:
+                    east(q, n, c).wait_send()
 
     per_parity(drain)
     for copy in sent.values():
@@ -257,7 +270,7 @@
             pltpu.SemaphoreType.DMA((chunks, lats - 1)),
         ],
         compiler_params=pltpu.CompilerParams(
-            collective_id=0, has_side_effects=True, vmem_limit_bytes=48 * 1024 * 1024
+            collective_id=0, has_side_effects=True, vmem_limit_bytes=63 * 1024 * 1024
         ),
         cost_estimate=pl.CostEstimate(
             flops=2 * offsets * layers * rows * cells * probes,

time: 25.4 us -> 26.9 us (1.059)
  Pallas kernels: 22.9 us -> 25 us
  local copies, waits for them, and re-layouts: 2.31 us -> 1.67 us
    pallas_call x1, Pallas kernels: 22.9 us -> 25 us  [per_device(): pl.pallas_call(functools.partial(sweep, lats, lons), out_shape=jax.ShapeD...]
    unnamed x5 -> x1, local copies, waits for them, and re-layouts: 2.31 us -> 1.67 us
where the time goes in v8:
time: 26.9 us; the launch traced here: 26.7 us
  Pallas kernels  25 us (93%)
  local copies, waits for them, and re-layouts  1.67 us (6%)
    pallas_call x1, Pallas kernels, per_device(): pl.pallas_call(functools.partial(sweep, lats, lons), out_shape=jax.ShapeD...  25 us
    unnamed x1, local copies, waits for them, and re-layouts  1.67 us

profile of v8, /device:TPU:1, one launch (start us, length us, event | category | flops | bytes accessed | tf_op | source)
XLA Modules:
  0.0 26.7 jit_solution(4548796220911542180)
XLA Ops:
  0.0 25.0 %shard_map.37 = f32[1,32,16,128]{3,2,1,0:T(8,128)} custom-call(bf16[32,16,128]{2,1,0:T(8,128)(2,1)} %res_hbm.1, f32[16,32]{1,0:T(8,128)} %bitcast.1, bf16[4,1,512,2048]{3,2,1,0:T(8,128)(2,1)} %panel_hbm.1), custom_call_target="tpu_custom_call" | custom-call | flops 1073741824 | bytes 8388608 | tf_op jit(solution)/shard_map/pallas_call | solution.py:249
  25.0 1.7 %copy.5 = f32[1,32,16,128]{3,2,1,0:T(8,128)} copy(f32[1,32,16,128]{3,2,1,0:T(8,128)} %shard_map.37) | data formatting | bytes 524288

commit v9 on v2

--- a/solution.py
+++ b/solution.py
@@ -10,15 +10,24 @@
 MESH = pl.DeviceIdType.MESH
 
 
-def route(offsets, lons):
-    if lons % 2 or offsets < 3:
-        table = {d: (-d, 0) for d in range(1, offsets)}
-        return 1, [table], list(range(1, offsets))
-    even, odd = {}, {}
-    for d in range(1, offsets):
-        even[d] = (1, 2) if d == 1 else (-2, d - 2)
-        odd[d] = (-1, d - 1) if d % 2 else (-2, d - 2)
-    return 2, [even, odd], list(range(2, offsets, 2)) + list(range(1, offsets, 2))
+def route(offsets, lons, chunks):
+    direct = {d: (-d, 0) for d in range(1, offsets)}
+    if lons % 2 or offsets < 3 or lons <= offsets:
+        return 1, [[direct] * chunks], list(range(1, offsets))
+    transit = offsets
+    even, odd = [], []
+    for c in range(chunks):
+        if c % 2:
+            even.append({**direct, 1: (-2, transit), 3: (-4, transit), transit: (1, 0)})
+            odd.append({**direct, 3: (-2, 1)})
+        else:
+            even.append({**direct, 1: (1, 2), 3: (1, transit)})
+            odd.append({**direct, 3: (-1, 2), transit: (-4, 0)})
+        if offsets == 3:
+            for table in (even[c], odd[c]):
+                if c % 2 == 0 or table is odd[c]:
+                    table.pop(transit, None)
+    return 2, [even, odd], [2] + [d for d in range(1, offsets) if d != 2]
 
 
 def sweep(
@@ -31,7 +40,7 @@
     chunks, part = outgoing.shape[0], outgoing.shape[3]
     band = cells // lats
     lat, lon = lax.axis_index("lat"), lax.axis_index("lon")
-    period, source, order = route(offsets, lons)
+    period, source, order = route(offsets, lons, chunks)
     pair = 2 if lats % 2 == 0 else 1
     groups = lats // pair
 
@@ -42,7 +51,7 @@
     loads = {}
     for d in [0] + order:
         loads[d] = pltpu.make_async_copy(panel_hbm.at[d], panel.at[d], panel_sem.at[d])
-        loads[d].start()
+    loads[0].start()
 
     def along(delta):
         return (lat, lax.rem(lon + (delta + lons), lons))
@@ -54,13 +63,23 @@
     partners = [(a, b) for a in range(groups - 1, -1, -1) for b in range(pair)][: lats]
     partners = [ab for ab in partners if ab != (0, 0)]
 
-    sends = [[] for _ in range(period)]
+    sends = [[[] for _ in range(chunks)] for _ in range(period)]
     senders = [set() for _ in range(period)]
+    passed = [set() for _ in range(period)]
     for q in range(period):
-        for d in order:
-            delta, held = source[q][d]
-            sends[(q + delta) % period].append((-delta, held, d))
-            senders[q].add(delta)
+        for c in range(chunks):
+            for d, (delta, held) in sorted(source[q][c].items()):
+                by = (q + delta) % period
+                sends[by][c].append((-delta, held, d))
+                senders[q].add(delta)
+                if held > 0:
+                    passed[by].add((held, c))
+
+    def urgency(q, c, send):
+        delta, _, d = send
+        return ((d, c) not in passed[(q + delta) % period], c)
+
+    receivers = [{send[0] for c in range(chunks) for send in sends[q][c]} for q in range(period)]
 
     def per_parity(action):
         for q in range(period):
@@ -91,7 +110,7 @@
         return pl.ds(c * part, part)
 
     def east(q, n, c):
-        delta, held, d = sends[q][n]
+        delta, held, d = sends[q][c][n]
         return pltpu.make_async_remote_copy(
             src_ref=blocks.at[held, chunk(c)],
             dst_ref=blocks.at[d, chunk(c)],
@@ -101,14 +120,15 @@
             device_id_type=MESH,
         )
 
-    def forward(held, cs):
-        def action(q):
-            for c in cs:
-                for n, send in enumerate(sends[q]):
-                    if send[1] == held:
-                        east(q, n, c).start()
-
-        per_parity(action)
+    def begin(q):
+        first = [
+            (urgency(q, c, send), n, c)
+            for c in range(chunks)
+            for n, send in enumerate(sends[q][c])
+            if send[1] == 0
+        ]
+        for _, n, c in sorted(first):
+            east(q, n, c).start()
 
     def arrive(d, c):
         pltpu.make_async_remote_copy(
@@ -120,8 +140,13 @@
             device_id_type=MESH,
         ).wait_recv()
 
-    pl.semaphore_wait(barrier, len(senders[0]) + len(partners))
-    forward(0, range(chunks))
+    def admit(q):
+        pl.semaphore_wait(barrier, len(receivers[q]) + len(partners))
+
+    per_parity(admit)
+    per_parity(begin)
+    for d in order:
+        loads[d].start()
 
     def accumulate(d, first):
         loads[d].wait()
@@ -136,10 +161,27 @@
                 total[l, :, cols] = value if first else total[l, :, cols] + value
 
     accumulate(0, True)
+    def relay(q):
+        for held, c in sorted(passed[q], key=lambda slot: (slot[0] != 2, slot[0])):
+            arrive(held, c)
+            for n, send in enumerate(sends[q][c]):
+                if send[1] == held:
+                    east(q, n, c).start()
+
+    def rest(d, c):
+        def action(q):
+            if (d, c) not in passed[q]:
+                arrive(d, c)
+
+        if all((d, c) not in passed[q] for q in range(period)):
+            arrive(d, c)
+        else:
+            per_parity(action)
+
+    per_parity(relay)
     for d in order[:-1]:
         for c in range(chunks):
-            arrive(d, c)
-            forward(d, [c])
+            rest(d, c)
         accumulate(d, False)
 
     last = order[-1]
@@ -158,7 +200,7 @@
 
     sent = {}
     for c in range(chunks):
-        arrive(last, c)
+        rest(last, c)
         for n, (a, b) in enumerate(partners):
             to = across(a, b)
             for l, value in enumerate(finish(c, to[0])):
@@ -187,7 +229,7 @@
 
     def drain(q):
         for c in range(chunks):
-            for n in range(len(sends[q])):
+            for n in range(len(sends[q][c])):
                 east(q, n, c).wait_send()
 
     per_parity(drain)
@@ -213,7 +255,7 @@
             pltpu.VMEM(residual.shape, jnp.bfloat16),
             pltpu.VMEM(noise_weights.shape[::-1], jnp.float32),
             pltpu.VMEM((offsets, layers, rows, cells), jnp.bfloat16),
-            pltpu.VMEM((offsets, probes, rows), jnp.bfloat16),
+            pltpu.VMEM((offsets + 1, probes, rows), jnp.bfloat16),
             pltpu.VMEM((layers, probes, cells), jnp.float32),
             pltpu.VMEM((chunks, lats - 1, layers, part, band), jnp.bfloat16),
             pltpu.VMEM((chunks, lats - 1, layers, part, band), jnp.bfloat16),
@@ -221,7 +263,7 @@
             pltpu.SemaphoreType.DMA((2,)),
             pltpu.SemaphoreType.DMA((offsets,)),
             pltpu.SemaphoreType.DMA((2 * offsets, chunks)),
-            pltpu.SemaphoreType.DMA((offsets, chunks)),
+            pltpu.SemaphoreType.DMA((offsets + 1, chunks)),
             pltpu.SemaphoreType.DMA((chunks, lats - 1)),
             pltpu.SemaphoreType.DMA((chunks, lats - 1)),
         ],

time: 25.6 us -> 25.5 us (level)
  no operation moved by 1% of the time
where the time goes in v9:
time: 25.5 us; the launch traced here: 25.3 us
  Pallas kernels  23.6 us (93%)
  local copies, waits for them, and re-layouts  1.67 us (7%)
    pallas_call x1, Pallas kernels, per_device(): pl.pallas_call(functools.partial(sweep, lats, lons), out_shape=jax.ShapeD...  23.6 us
    unnamed x1, local copies, waits for them, and re-layouts  1.67 us

profile of v9, /device:TPU:1, one launch (start us, length us, event | category | flops | bytes accessed | tf_op | source)
XLA Modules:
  0.0 25.3 jit_solution(8020456161664899559)
XLA Ops:
  0.0 23.6 %shard_map.37 = f32[1,32,16,128]{3,2,1,0:T(8,128)} custom-call(bf16[32,16,128]{2,1,0:T(8,128)(2,1)} %res_hbm.1, f32[16,32]{1,0:T(8,128)} %bitcast.1, bf16[4,1,512,2048]{3,2,1,0:T(8,128)(2,1)} %panel_hbm.1), custom_call_target="tpu_custom_call" | custom-call | flops 1073741824 | bytes 8388608 | tf_op jit(solution)/shard_map/pallas_call | solution.py:247
  23.7 1.7 %copy.5 = f32[1,32,16,128]{3,2,1,0:T(8,128)} copy(f32[1,32,16,128]{3,2,1,0:T(8,128)} %shard_map.37) | data formatting | bytes 524288

commit v10 on v9

--- a/solution.py
+++ b/solution.py
@@ -32,12 +32,12 @@
 
 def sweep(
     lats, lons, res_hbm, nw_hbm, panel_hbm, out_ref,
-    res, nw, panel, blocks, total, outgoing, incoming, summed,
+    res, nw, panel, blocks, total, outgoing, incoming,
     input_sem, panel_sem, east_send, east_recv, band_send, band_recv,
 ):
     offsets, layers, rows, cells = panel_hbm.shape
     probes = res_hbm.shape[-1]
-    chunks, part = outgoing.shape[0], outgoing.shape[3]
+    chunks, part = blocks.shape[1], blocks.shape[2]
     band = cells // lats
     lat, lon = lax.axis_index("lat"), lax.axis_index("lon")
     period, source, order = route(offsets, lons, chunks)
@@ -104,16 +104,14 @@
     pieces = [
         nw[:, y : y + 1] * res[y].astype(jnp.float32) for y in range(rows // columns)
     ]
-    blocks[0] = jnp.concatenate(pieces, axis=0).T.astype(jnp.bfloat16)
-
-    def chunk(c):
-        return pl.ds(c * part, part)
+    weighted = jnp.concatenate(pieces, axis=0).astype(jnp.bfloat16)
+    blocks[0] = weighted.reshape(chunks, part, probes)
 
     def east(q, n, c):
         delta, held, d = sends[q][c][n]
         return pltpu.make_async_remote_copy(
-            src_ref=blocks.at[held, chunk(c)],
-            dst_ref=blocks.at[d, chunk(c)],
+            src_ref=blocks.at[held, c],
+            dst_ref=blocks.at[d, c],
             send_sem=east_send.at[n, c],
             recv_sem=east_recv.at[d, c],
             device_id=along(delta),
@@ -132,8 +130,8 @@
 
     def arrive(d, c):
         pltpu.make_async_remote_copy(
-            src_ref=blocks.at[d, chunk(c)],
-            dst_ref=blocks.at[d, chunk(c)],
+            src_ref=blocks.at[d, c],
+            dst_ref=blocks.at[d, c],
             send_sem=east_send.at[0, c],
             recv_sem=east_recv.at[d, c],
             device_id=along(1),
@@ -148,17 +146,19 @@
     for d in order:
         loads[d].start()
 
+    def product(d, l, cols):
+        return lax.dot_general(
+            panel[d, l, :, cols], blocks[d].reshape(rows, probes),
+            (((0,), (0,)), ((), ())), preferred_element_type=jnp.float32,
+        )
+
     def accumulate(d, first):
         loads[d].wait()
         for l in range(layers):
-
-            @pl.loop(0, lats)
-            def _(b):
-                cols = pl.ds(pl.multiple_of(b * band, band), band)
-                value = jnp.dot(
-                    blocks[d], panel[d, l, :, cols], preferred_element_type=jnp.float32
-                )
-                total[l, :, cols] = value if first else total[l, :, cols] + value
+            for b in range(lats):
+                cols = pl.ds(b * band, band)
+                value = product(d, l, cols)
+                total[l, cols] = value if first else total[l, cols] + value
 
     accumulate(0, True)
     def relay(q):
@@ -187,45 +187,34 @@
     last = order[-1]
     loads[last].wait()
 
-    def finish(c, to):
-        cols = pl.ds(pl.multiple_of(to * band, band), band)
-        return [
-            total[l, chunk(c), cols]
-            + jnp.dot(
-                blocks[last, chunk(c)], panel[last, l, :, cols],
-                preferred_element_type=jnp.float32,
-            )
-            for l in range(layers)
-        ]
-
-    sent = {}
     for c in range(chunks):
         rest(last, c)
-        for n, (a, b) in enumerate(partners):
-            to = across(a, b)
-            for l, value in enumerate(finish(c, to[0])):
-                outgoing[c, n, l] = value.astype(jnp.bfloat16)
-            sent[c, n] = pltpu.make_async_remote_copy(
-                src_ref=outgoing.at[c, n],
-                dst_ref=incoming.at[c, n],
-                send_sem=band_send.at[c, n],
-                recv_sem=band_recv.at[c, n],
-                device_id=to,
-                device_id_type=MESH,
-            )
-            sent[c, n].start()
-        for l, value in enumerate(finish(c, lat)):
-            summed[l, chunk(c)] = value
-    for c in range(chunks):
-        for n in reversed(range(len(partners))):
-            sent[c, n].wait_recv()
-        for l in range(layers):
-            value = summed[l, chunk(c)]
-            for n in range(len(partners)):
-                value = value + incoming[c, n, l].astype(jnp.float32)
-            summed[l, chunk(c)] = value
-    for l in range(layers):
-        out_ref[l] = summed[l].T.reshape(out_ref.shape[1:])
+
+    def finish(to):
+        cols = pl.ds(pl.multiple_of(to * band, band), band)
+        return [total[l, cols] + product(last, l, cols) for l in range(layers)]
+
+    sent = []
+    for n, (a, b) in enumerate(partners):
+        to = across(a, b)
+        for l, value in enumerate(finish(to[0])):
+            outgoing[n, l] = value.astype(jnp.bfloat16)
+        copy = pltpu.make_async_remote_copy(
+            src_ref=outgoing.at[n],
+            dst_ref=incoming.at[n],
+            send_sem=band_send.at[n],
+            recv_sem=band_recv.at[n],
+            device_id=to,
+            device_id_type=MESH,
+        )
+        copy.start()
+        sent.append(copy)
+    mine = finish(lat)
+    for n, copy in reversed(list(enumerate(sent))):
+        copy.wait_recv()
+        mine = [value + incoming[n, l].astype(jnp.float32) for l, value in enumerate(mine)]
+    for l, value in enumerate(mine):
+        out_ref[l] = value.reshape(out_ref.shape[1:])
 
     def drain(q):
         for c in range(chunks):
@@ -233,7 +222,7 @@
                 east(q, n, c).wait_send()
 
     per_parity(drain)
-    for copy in sent.values():
+    for copy in sent:
         copy.wait_send()
 
 
@@ -241,8 +230,7 @@
     offsets, layers, rows, cells = kernel.shape
     probes = residual.shape[2]
     band = cells // lats
-    chunks = 2 if probes % 32 == 0 else 1
-    part = probes // chunks
+    chunks = 2 if rows % 32 == 0 else 1
     remote = pl.BlockSpec(memory_space=pltpu.HBM)
     return pl.pallas_call(
         functools.partial(sweep, lats, lons),
@@ -255,17 +243,16 @@
             pltpu.VMEM(residual.shape, jnp.bfloat16),
             pltpu.VMEM(noise_weights.shape[::-1], jnp.float32),
             pltpu.VMEM((offsets, layers, rows, cells), jnp.bfloat16),
-            pltpu.VMEM((offsets + 1, probes, rows), jnp.bfloat16),
-            pltpu.VMEM((layers, probes, cells), jnp.float32),
-            pltpu.VMEM((chunks, lats - 1, layers, part, band), jnp.bfloat16),
-            pltpu.VMEM((chunks, lats - 1, layers, part, band), jnp.bfloat16),
-            pltpu.VMEM((layers, probes, band), jnp.float32),
+            pltpu.VMEM((offsets + 1, chunks, rows // chunks, probes), jnp.bfloat16),
+            pltpu.VMEM((layers, cells, probes), jnp.float32),
+            pltpu.VMEM((lats - 1, layers, band, probes), jnp.bfloat16),
+            pltpu.VMEM((lats - 1, layers, band, probes), jnp.bfloat16),
             pltpu.SemaphoreType.DMA((2,)),
             pltpu.SemaphoreType.DMA((offsets,)),
             pltpu.SemaphoreType.DMA((2 * offsets, chunks)),
             pltpu.SemaphoreType.DMA((offsets + 1, chunks)),
-            pltpu.SemaphoreType.DMA((chunks, lats - 1)),
-            pltpu.SemaphoreType.DMA((chunks, lats - 1)),
+            pltpu.SemaphoreType.DMA((lats - 1,)),
+            pltpu.SemaphoreType.DMA((lats - 1,)),
         ],
         compiler_params=pltpu.CompilerParams(
             collective_id=0, has_side_effects=True, vmem_limit_bytes=63 * 1024 * 1024

time: 25.5 us -> 25.4 us (level)
  no operation moved by 1% of the time
where the time goes in v10:
time: 25.4 us; the launch traced here: 25.3 us
  Pallas kernels  23.6 us (93%)
  local copies, waits for them, and re-layouts  1.67 us (7%)
    pallas_call x1, Pallas kernels, per_device(): pl.pallas_call(functools.partial(sweep, lats, lons), out_shape=jax.ShapeD...  23.6 us
    unnamed x1, local copies, waits for them, and re-layouts  1.67 us

profile of v10, /device:TPU:1, one launch (start us, length us, event | category | flops | bytes accessed | tf_op | source)
XLA Modules:
  0.0 25.3 jit_solution(3861970651439968035)
XLA Ops:
  0.0 23.6 %shard_map.37 = f32[1,32,16,128]{3,2,1,0:T(8,128)} custom-call(bf16[32,16,128]{2,1,0:T(8,128)(2,1)} %res_hbm.1, f32[16,32]{1,0:T(8,128)} %bitcast.1, bf16[4,1,512,2048]{3,2,1,0:T(8,128)(2,1)} %panel_hbm.1), custom_call_target="tpu_custom_call" | custom-call | flops 1073741824 | bytes 8388608 | tf_op jit(solution)/shard_map/pallas_call | solution.py:235
  23.6 1.7 %copy.5 = f32[1,32,16,128]{3,2,1,0:T(8,128)} copy(f32[1,32,16,128]{3,2,1,0:T(8,128)} %shard_map.37) | data formatting | bytes 524288

commit v11 on v10

--- a/solution.py
+++ b/solution.py
@@ -49,9 +49,15 @@
     res_load.start()
     nw_load.start()
     loads = {}
+    pieces = 8 if rows % 128 == 0 else 1
     for d in [0] + order:
         loads[d] = pltpu.make_async_copy(panel_hbm.at[d], panel.at[d], panel_sem.at[d])
-    loads[0].start()
+        for n in range(pieces):
+            for l in range(layers):
+                some = pl.ds(n * (rows // pieces), rows // pieces)
+                pltpu.make_async_copy(
+                    panel_hbm.at[d, l, some], panel.at[d, l, some], panel_sem.at[d]
+                ).start()
 
     def along(delta):
         return (lat, lax.rem(lon + (delta + lons), lons))
@@ -143,8 +149,6 @@
 
     per_parity(admit)
     per_parity(begin)
-    for d in order:
-        loads[d].start()
 
     def product(d, l, cols):
         return lax.dot_general(

time: 25.4 us -> 27.6 us (1.087)
  Pallas kernels: 23.6 us -> 25.7 us
    pallas_call x1, Pallas kernels: 23.6 us -> 25.7 us  [per_device(): pl.pallas_call(functools.partial(sweep, lats, lons), out_shape=jax.ShapeD...]
where the time goes in v11:
time: 27.6 us; the launch traced here: 27.4 us
  Pallas kernels  25.7 us (93%)
  local copies, waits for them, and re-layouts  1.67 us (6%)
    pallas_call x1, Pallas kernels, per_device(): pl.pallas_call(functools.partial(sweep, lats, lons), out_shape=jax.ShapeD...  25.7 us
    unnamed x1, local copies, waits for them, and re-layouts  1.67 us

profile of v11, /device:TPU:1, one launch (start us, length us, event | category | flops | bytes accessed | tf_op | source)
XLA Modules:
  0.0 27.4 jit_solution(1991638388839899440)
XLA Ops:
  0.0 25.7 %shard_map.37 = f32[1,32,16,128]{3,2,1,0:T(8,128)} custom-call(bf16[32,16,128]{2,1,0:T(8,128)(2,1)} %res_hbm.1, f32[16,32]{1,0:T(8,128)} %bitcast.1, bf16[4,1,512,2048]{3,2,1,0:T(8,128)(2,1)} %panel_hbm.1), custom_call_target="tpu_custom_call" | custom-call | flops 1073741824 | bytes 8388608 | tf_op jit(solution)/shard_map/pallas_call | solution.py:239
  25.8 1.7 %copy.5 = f32[1,32,16,128]{3,2,1,0:T(8,128)} copy(f32[1,32,16,128]{3,2,1,0:T(8,128)} %shard_map.37) | data formatting | bytes 524288

commit v12 on v10

--- a/solution.py
+++ b/solution.py
@@ -143,8 +143,7 @@
 
     per_parity(admit)
     per_parity(begin)
-    for d in order:
-        loads[d].start()
+    loads[order[0]].start()
 
     def product(d, l, cols):
         return lax.dot_general(
@@ -179,6 +178,8 @@
             per_parity(action)
 
     per_parity(relay)
+    for d in order[1:]:
+        loads[d].start()
     for d in order[:-1]:
         for c in range(chunks):
             rest(d, c)

time: 25.4 us -> 25.4 us (level)
  no operation moved by 1% of the time
where the time goes in v12:
time: 25.4 us; the launch traced here: 25.3 us
  Pallas kernels  23.6 us (93%)
  local copies, waits for them, and re-layouts  1.67 us (7%)
    pallas_call x1, Pallas kernels, per_device(): pl.pallas_call(functools.partial(sweep, lats, lons), out_shape=jax.ShapeD...  23.6 us
    unnamed x1, local copies, waits for them, and re-layouts  1.67 us

profile of v12, /device:TPU:1, one launch (start us, length us, event | category | flops | bytes accessed | tf_op | source)
XLA Modules:
  0.0 25.3 jit_solution(1571174754217008458)
XLA Ops:
  0.0 23.6 %shard_map.37 = f32[1,32,16,128]{3,2,1,0:T(8,128)} custom-call(bf16[32,16,128]{2,1,0:T(8,128)(2,1)} %res_hbm.1, f32[16,32]{1,0:T(8,128)} %bitcast.1, bf16[4,1,512,2048]{3,2,1,0:T(8,128)(2,1)} %panel_hbm.1), custom_call_target="tpu_custom_call" | custom-call | flops 1073741824 | bytes 8388608 | tf_op jit(solution)/shard_map/pallas_call | solution.py:236
  23.6 1.7 %copy.5 = f32[1,32,16,128]{3,2,1,0:T(8,128)} copy(f32[1,32,16,128]{3,2,1,0:T(8,128)} %shard_map.37) | data formatting | bytes 524288

commit v13 on v12

--- a/solution.py
+++ b/solution.py
@@ -32,8 +32,8 @@
 
 def sweep(
     lats, lons, res_hbm, nw_hbm, panel_hbm, out_ref,
-    res, nw, panel, blocks, total, outgoing, incoming,
-    input_sem, panel_sem, east_send, east_recv, band_send, band_recv,
+    res, nw, panel, blocks, total, chip_out, chip_in, band_out, band_in,
+    input_sem, panel_sem, east_send, east_recv, chip_send, chip_recv, band_send, band_recv,
 ):
     offsets, layers, rows, cells = panel_hbm.shape
     probes = res_hbm.shape[-1]
@@ -60,8 +60,7 @@
         to = lax.rem(lat // pair + a, groups) * pair + lax.rem(lat % pair + b, pair)
         return (to, lon)
 
-    partners = [(a, b) for a in range(groups - 1, -1, -1) for b in range(pair)][: lats]
-    partners = [ab for ab in partners if ab != (0, 0)]
+    partners = [(a, 0) for a in range(1, groups)] + [(0, b) for b in range(1, pair)]
 
     sends = [[[] for _ in range(chunks)] for _ in range(period)]
     senders = [set() for _ in range(period)]
@@ -195,25 +194,57 @@
         cols = pl.ds(pl.multiple_of(to * band, band), band)
         return [total[l, cols] + product(last, l, cols) for l in range(layers)]
 
-    sent = []
-    for n, (a, b) in enumerate(partners):
-        to = across(a, b)
-        for l, value in enumerate(finish(to[0])):
-            outgoing[n, l] = value.astype(jnp.bfloat16)
-        copy = pltpu.make_async_remote_copy(
-            src_ref=outgoing.at[n],
-            dst_ref=incoming.at[n],
-            send_sem=band_send.at[n],
-            recv_sem=band_recv.at[n],
-            device_id=to,
+    def inner(a, b):
+        return pltpu.make_async_remote_copy(
+            src_ref=chip_out.at[a, b - 1],
+            dst_ref=chip_in.at[a, b - 1],
+            send_sem=chip_send.at[a, b - 1],
+            recv_sem=chip_recv.at[a, b - 1],
+            device_id=across(0, b),
             device_id_type=MESH,
         )
-        copy.start()
-        sent.append(copy)
-    mine = finish(lat)
-    for n, copy in reversed(list(enumerate(sent))):
-        copy.wait_recv()
-        mine = [value + incoming[n, l].astype(jnp.float32) for l, value in enumerate(mine)]
+
+    def outer(a):
+        return pltpu.make_async_remote_copy(
+            src_ref=band_out.at[a - 1],
+            dst_ref=band_in.at[a - 1],
+            send_sem=band_send.at[a - 1],
+            recv_sem=band_recv.at[a - 1],
+            device_id=across(a, 0),
+            device_id_type=MESH,
+        )
+
+    def offer(a):
+        for b in range(1, pair):
+            for l, value in enumerate(finish(across(a, b)[0])):
+                chip_out[a, b - 1, l] = value.astype(jnp.bfloat16)
+            inner(a, b).start()
+
+    def collect(a, values):
+        for b in range(1, pair):
+            inner(a, b).wait_recv()
+            values = [
+                value + chip_in[a, b - 1, l].astype(jnp.float32)
+                for l, value in enumerate(values)
+            ]
+        return values
+
+    steps = list(range(1, groups)) + [0]
+    offer(steps[0])
+    for n, a in enumerate(steps):
+        mine = finish(across(a, 0)[0])
+        if n + 1 < groups:
+            offer(steps[n + 1])
+        mine = collect(a, mine)
+        if a > 0:
+            for l, value in enumerate(mine):
+                band_out[a - 1, l] = value.astype(jnp.bfloat16)
+            outer(a).start()
+    for a in range(1, groups):
+        outer(a).wait_recv()
+        mine = [
+            value + band_in[a - 1, l].astype(jnp.float32) for l, value in enumerate(mine)
+        ]
     for l, value in enumerate(mine):
         out_ref[l] = value.reshape(out_ref.shape[1:])
 
@@ -223,8 +254,11 @@
                 east(q, n, c).wait_send()
 
     per_parity(drain)
-    for copy in sent:
-        copy.wait_send()
+    for a in range(groups):
+        for b in range(1, pair):
+            inner(a, b).wait_send()
+        if a > 0:
+            outer(a).wait_send()
 
 
 def per_device(lats, lons, residual, noise_weights, kernel):
@@ -232,6 +266,9 @@
     probes = residual.shape[2]
     band = cells // lats
     chunks = 2 if rows % 32 == 0 else 1
+    pair = 2 if lats % 2 == 0 else 1
+    groups = lats // pair
+    inner, outer = max(pair - 1, 1), max(groups - 1, 1)
     remote = pl.BlockSpec(memory_space=pltpu.HBM)
     return pl.pallas_call(
         functools.partial(sweep, lats, lons),
@@ -246,14 +283,18 @@
             pltpu.VMEM((offsets, layers, rows, cells), jnp.bfloat16),
             pltpu.VMEM((offsets + 1, chunks, rows // chunks, probes), jnp.bfloat16),
             pltpu.VMEM((layers, cells, probes), jnp.float32),
-            pltpu.VMEM((lats - 1, layers, band, probes), jnp.bfloat16),
-            pltpu.VMEM((lats - 1, layers, band, probes), jnp.bfloat16),
+            pltpu.VMEM((groups, inner, layers, band, probes), jnp.bfloat16),
+            pltpu.VMEM((groups, inner, layers, band, probes), jnp.bfloat16),
+            pltpu.VMEM((outer, layers, band, probes), jnp.bfloat16),
+            pltpu.VMEM((outer, layers, band, probes), jnp.bfloat16),
             pltpu.SemaphoreType.DMA((2,)),
             pltpu.SemaphoreType.DMA((offsets,)),
             pltpu.SemaphoreType.DMA((2 * offsets, chunks)),
             pltpu.SemaphoreType.DMA((offsets + 1, chunks)),
-            pltpu.SemaphoreType.DMA((lats - 1,)),
-            pltpu.SemaphoreType.DMA((lats - 1,)),
+            pltpu.SemaphoreType.DMA((groups, inner)),
+            pltpu.SemaphoreType.DMA((groups, inner)),
+            pltpu.SemaphoreType.DMA((outer,)),
+            pltpu.SemaphoreType.DMA((outer,)),
         ],
         compiler_params=pltpu.CompilerParams(
             collective_id=0, has_side_effects=True, vmem_limit_bytes=63 * 1024 * 1024

time: 25.4 us -> 26.4 us (1.039); the launches traced: 25.3 us -> 25.9 us
  Pallas kernels: 23.6 us -> 24.2 us
    pallas_call x1, Pallas kernels: 23.6 us -> 24.2 us  [per_device(): pl.pallas_call(functools.partial(sweep, lats, lons), out_shape=jax.ShapeD...]
where the time goes in v13:
time: 26.4 us; the launch traced here: 25.9 us
  Pallas kernels  24.2 us (92%)
  local copies, waits for them, and re-layouts  1.67 us (6%)
    pallas_call x1, Pallas kernels, per_device(): pl.pallas_call(functools.partial(sweep, lats, lons), out_shape=jax.ShapeD...  24.2 us
    unnamed x1, local copies, waits for them, and re-layouts  1.67 us

profile of v13, /device:TPU:1, one launch (start us, length us, event | category | flops | bytes accessed | tf_op | source)
XLA Modules:
  0.0 25.9 jit_solution(1297312860046836213)
XLA Ops:
  0.0 24.2 %shard_map.37 = f32[1,32,16,128]{3,2,1,0:T(8,128)} custom-call(bf16[32,16,128]{2,1,0:T(8,128)(2,1)} %res_hbm.1, f32[16,32]{1,0:T(8,128)} %bitcast.1, bf16[4,1,512,2048]{3,2,1,0:T(8,128)(2,1)} %panel_hbm.1), custom_call_target="tpu_custom_call" | custom-call | flops 1073741824 | bytes 8388608 | tf_op jit(solution)/shard_map/pallas_call | solution.py:273
  24.2 1.7 %copy.5 = f32[1,32,16,128]{3,2,1,0:T(8,128)} copy(f32[1,32,16,128]{3,2,1,0:T(8,128)} %shard_map.37) | data formatting | bytes 524288

commit v14 on v12

--- a/solution.py
+++ b/solution.py
@@ -51,7 +51,6 @@
     loads = {}
     for d in [0] + order:
         loads[d] = pltpu.make_async_copy(panel_hbm.at[d], panel.at[d], panel_sem.at[d])
-    loads[0].start()
 
     def along(delta):
         return (lat, lax.rem(lon + (delta + lons), lons))
@@ -143,6 +142,7 @@
 
     per_parity(admit)
     per_parity(begin)
+    loads[0].start()
     loads[order[0]].start()
 
     def product(d, l, cols):

time: 25.4 us -> 25.4 us (level)
  no operation moved by 1% of the time
where the time goes in v14:
time: 25.4 us; the launch traced here: 25.3 us
  Pallas kernels  23.6 us (93%)
  local copies, waits for them, and re-layouts  1.67 us (7%)
    pallas_call x1, Pallas kernels, per_device(): pl.pallas_call(functools.partial(sweep, lats, lons), out_shape=jax.ShapeD...  23.6 us
    unnamed x1, local copies, waits for them, and re-layouts  1.67 us

profile of v14, /device:TPU:1, one launch (start us, length us, event | category | flops | bytes accessed | tf_op | source)
XLA Modules:
  0.0 25.3 jit_solution(8110363057330060700)
XLA Ops:
  0.0 23.6 %shard_map.37 = f32[1,32,16,128]{3,2,1,0:T(8,128)} custom-call(bf16[32,16,128]{2,1,0:T(8,128)(2,1)} %res_hbm.1, f32[16,32]{1,0:T(8,128)} %bitcast.1, bf16[4,1,512,2048]{3,2,1,0:T(8,128)(2,1)} %panel_hbm.1), custom_call_target="tpu_custom_call" | custom-call | flops 1073741824 | bytes 8388608 | tf_op jit(solution)/shard_map/pallas_call | solution.py:236
  23.6 1.7 %copy.5 = f32[1,32,16,128]{3,2,1,0:T(8,128)} copy(f32[1,32,16,128]{3,2,1,0:T(8,128)} %shard_map.37) | data formatting | bytes 524288

commit v15 on v12

--- a/solution.py
+++ b/solution.py
@@ -27,7 +27,7 @@
             for table in (even[c], odd[c]):
                 if c % 2 == 0 or table is odd[c]:
                     table.pop(transit, None)
-    return 2, [even, odd], [2] + [d for d in range(1, offsets) if d != 2]
+    return 2, [even, odd], [2] + [d for d in range(offsets - 1, 0, -1) if d != 2]
 
 
 def sweep(

time: 25.4 us -> 26.2 us (1.031)
  Pallas kernels: 23.6 us -> 24.3 us
    pallas_call x1, Pallas kernels: 23.6 us -> 24.3 us  [per_device(): pl.pallas_call(functools.partial(sweep, lats, lons), out_shape=jax.ShapeD...]
where the time goes in v15:
time: 26.2 us; the launch traced here: 26 us
  Pallas kernels  24.3 us (93%)
  local copies, waits for them, and re-layouts  1.67 us (6%)
    pallas_call x1, Pallas kernels, per_device(): pl.pallas_call(functools.partial(sweep, lats, lons), out_shape=jax.ShapeD...  24.3 us
    unnamed x1, local copies, waits for them, and re-layouts  1.67 us

profile of v15, /device:TPU:1, one launch (start us, length us, event | category | flops | bytes accessed | tf_op | source)
XLA Modules:
  0.0 26.0 jit_solution(12758326437134521600)
XLA Ops:
  0.0 24.3 %shard_map.37 = f32[1,32,16,128]{3,2,1,0:T(8,128)} custom-call(bf16[32,16,128]{2,1,0:T(8,128)(2,1)} %res_hbm.1, f32[16,32]{1,0:T(8,128)} %bitcast.1, bf16[4,1,512,2048]{3,2,1,0:T(8,128)(2,1)} %panel_hbm.1), custom_call_target="tpu_custom_call" | custom-call | flops 1073741824 | bytes 8388608 | tf_op jit(solution)/shard_map/pallas_call | solution.py:236
  24.3 1.7 %copy.5 = f32[1,32,16,128]{3,2,1,0:T(8,128)} copy(f32[1,32,16,128]{3,2,1,0:T(8,128)} %shard_map.37) | data formatting | bytes 524288
